TPU v7x, 32 devices: a whole 2x2x4 slice. The times are simulated.
32 devices in a mesh: fsdp: 8 (over z, core), dp: 4 (over y, x).
Axes of the slice: x: 2, y: 2, z: 4, core: 2. Of those that a mesh axis runs over, the one named last changes fastest.
Arguments:
- target_x: bfloat16 [512, 4096], P('dp'), may hold values from -6 to 6
- target_y: bfloat16 [512, 4096], P('dp'), may hold values from -6 to 6
- poison_x: bfloat16 [1024, 4096], P('dp'), may hold values from -6 to 6
- poison_y: bfloat16 [1024, 4096], P('dp'), may hold values from -6 to 6
- w_gate: bfloat16 [4096, 7168], P(None, 'fsdp'), as said below
- w_up: bfloat16 [4096, 7168], P(None, 'fsdp'), as said below
- w_down: bfloat16 [7168, 4096], P('fsdp'), may hold values from -0.0625 to 0.0625
Outputs:
- poison_step: float32 [1024, 4096], P('dp', 'fsdp')
- alignment: float32 [], replicated
Inputs may be any that keep to these rules, and one draw needn't show every extreme that they name: `w_gate`: a weight matrix whose entries have mean 0 and a root mean square near 4096 ** -0.5. `w_up`: a weight matrix whose entries have mean 0 and a root mean square near 4096 ** -0.5.
All inputs are finite; a program needn't handle non-finite values.
Results may differ from a plain program's by a relative error of at most 0.02.
Values may be sent and summed in bfloat16 or wider, within the bound.
A program may use at most 192 MiB of HBM per device.

v0:
```python
import jax
import jax.numpy as jnp
from jax import lax
from jax.sharding import PartitionSpec as P

EPSILON = 1e-06


def silu_parts(preact):
    sigma = jax.nn.sigmoid(preact)
    silu_val = preact * sigma
    slope = sigma * (1.0 + preact * (1.0 - sigma))
    curve = sigma * (1.0 - sigma) * (2.0 + preact * (1.0 - 2.0 * sigma))
    return (silu_val, slope, curve)


def matmul(left, right):
    return jnp.dot(left, right, preferred_element_type=jnp.float32)


def inner_rows(left, right):
    return lax.dot_general(
        left, right, (((0,), (0,)), ((), ())), preferred_element_type=jnp.float32
    )


def inner_cols(left, right):
    return lax.dot_general(
        left, right, (((1,), (1,)), ((), ())), preferred_element_type=jnp.float32
    )


def mlp_forward(inputs, w_gate, w_up, w_down):
    gate_pre = matmul(inputs, w_gate)
    upper = matmul(inputs, w_up)
    silu_val, slope, curve = silu_parts(gate_pre)
    hidden = (silu_val * upper).astype(jnp.bfloat16)
    return (upper, silu_val, slope, curve, hidden, matmul(hidden, w_down))


def backward(inputs, labels, output, upper, silu_val, slope, w_down, token_total):
    error = (
        (inputs.astype(jnp.float32) + output - labels.astype(jnp.float32)) / token_total
    ).astype(jnp.bfloat16)
    back_hidden = inner_cols(error, w_down)
    gate_back = (back_hidden * upper * slope).astype(jnp.bfloat16)
    upper_back = (back_hidden * silu_val).astype(jnp.bfloat16)
    return (error, back_hidden, gate_back, upper_back)


def grad_rows(inputs, error, hidden, gate_back, upper_back):
    return jnp.concatenate(
        [inner_rows(inputs, gate_back), inner_rows(inputs, upper_back), inner_rows(error, hidden)],
        axis=1,
    )


def local(target_x, target_y, poison_x, poison_y, w_gate, w_up, w_down):
    hidden_width = w_gate.shape[1]
    model_width = w_gate.shape[0]
    dp_size = lax.axis_size("dp")
    tgt_total = target_x.shape[0] * dp_size
    poi_total = poison_x.shape[0] * dp_size
    upper_tgt, silu_tgt, slope_tgt, curve_tgt, hidden_tgt, part_tgt = mlp_forward(
        target_x, w_gate, w_up, w_down
    )
    output_tgt = lax.psum(part_tgt.astype(jnp.bfloat16), "fsdp").astype(jnp.float32)
    error_tgt, back_tgt, gback_tgt, uback_tgt = backward(
        target_x, target_y, output_tgt, upper_tgt, silu_tgt, slope_tgt, w_down, tgt_total
    )
    upper_poi, silu_poi, slope_poi, curve_poi, hidden_poi, part_poi = mlp_forward(
        poison_x, w_gate, w_up, w_down
    )
    output_poi = lax.psum(part_poi.astype(jnp.bfloat16), "fsdp").astype(jnp.float32)
    error_poi, back_poi, gback_poi, uback_poi = backward(
        poison_x, poison_y, output_poi, upper_poi, silu_poi, slope_poi, w_down, poi_total
    )
    joint = lax.psum_scatter(
        jnp.concatenate(
            [
                grad_rows(target_x, error_tgt, hidden_tgt, gback_tgt, uback_tgt),
                grad_rows(poison_x, error_poi, hidden_poi, gback_poi, uback_poi),
            ],
            axis=1,
        ).astype(jnp.bfloat16),
        "dp",
        scatter_dimension=0,
        tiled=True,
    ).astype(jnp.float32)
    grad_tgt = joint[:, : 3 * hidden_width]
    grad_poi = joint[:, 3 * hidden_width :]
    norm_tt, norm_pp, cross_tp = lax.psum(
        (jnp.sum(grad_tgt * grad_tgt), jnp.sum(grad_poi * grad_poi), jnp.sum(grad_tgt * grad_poi)),
        ("fsdp", "dp"),
    )
    length_tgt = jnp.sqrt(norm_tt + EPSILON)
    length_poi = jnp.sqrt(norm_pp + EPSILON)
    denom = length_tgt * length_poi
    alignment = 1.0 - cross_tp / denom
    coef_tgt = -1.0 / denom
    coef_poi = cross_tp / (denom * length_poi * length_poi)
    local_sens = (coef_tgt * grad_tgt + coef_poi * grad_poi).astype(jnp.bfloat16)
    sens_full = lax.all_gather(local_sens, "dp", axis=0, tiled=True)
    v_gate = sens_full[:, :hidden_width]
    v_upper = sens_full[:, hidden_width : 2 * hidden_width]
    v_down = sens_full[:, 2 * hidden_width :]
    tan_gate = matmul(poison_x, v_gate)
    tan_upper = matmul(poison_x, v_upper)
    hidden_tan = (slope_poi * tan_gate * upper_poi + silu_poi * tan_upper).astype(jnp.bfloat16)
    part_tan = matmul(hidden_tan, w_down) + inner_cols(hidden_poi, v_down)
    output_tan = lax.psum(part_tan.astype(jnp.bfloat16), "fsdp").astype(jnp.float32)
    back_tan = (output_tan / poi_total).astype(jnp.bfloat16)
    mixed = inner_cols(back_tan, w_down) + matmul(error_poi, v_down)
    gate_total = (
        mixed * upper_poi * slope_poi
        + back_poi * (curve_poi * tan_gate * upper_poi + slope_poi * tan_upper)
    ).astype(jnp.bfloat16)
    upper_total = (mixed * silu_poi + back_poi * slope_poi * tan_gate).astype(jnp.bfloat16)
    gate_dir = (back_poi * slope_poi * upper_poi).astype(jnp.bfloat16)
    upper_dir = (back_poi * silu_poi).astype(jnp.bfloat16)
    part_grad = (
        inner_cols(gate_total, w_gate)
        + inner_cols(upper_total, w_up)
        + inner_cols(gate_dir, v_gate)
        + inner_cols(upper_dir, v_upper)
    )
    grad_cols = lax.psum_scatter(
        part_grad.astype(jnp.bfloat16), "fsdp", scatter_dimension=1, tiled=True
    ).astype(jnp.float32)
    columns = grad_cols.shape[1]
    residual_cols = lax.dynamic_slice_in_dim(
        back_tan, lax.axis_index("fsdp") * columns, columns, 1
    ).astype(jnp.float32)
    scaled = (grad_cols + residual_cols) * float(poi_total * model_width)
    total_sq = lax.psum(jnp.sum(scaled * scaled), ("fsdp", "dp"))
    mean_sq = total_sq / float(poi_total * model_width)
    return (scaled * lax.rsqrt(mean_sq + EPSILON), alignment)


def solution(mesh):
    in_specs = (
        P("dp", None),
        P("dp", None),
        P("dp", None),
        P("dp", None),
        P(None, "fsdp"),
        P(None, "fsdp"),
        P("fsdp", None),
    )
    out_specs = (P("dp", "fsdp"), P())
    return jax.shard_map(local, mesh=mesh, in_specs=in_specs, out_specs=out_specs, check_vma=False)
```

profile of v0, /device:TPU:0, one launch (start us, length us, event | category | flops | bytes accessed | tf_op | source)
XLA Modules:
  0.0 999.4 jit_solution(9322678073269802209)
XLA Ops:
  7.2 0.0 all-reduce.7.cloned.1.call-start
  7.2 6.2 fusion.70
  13.5 1.3 fusion.71
  14.8 2.1 copy-done.1
  16.9 0.6 copy-done.7
  17.5 3.3 multiply_convert_fusion.6
  20.8 1.3 multiply_convert_fusion.11
  22.1 3.7 convolution_convert_fusion
  25.8 2.2 convolution_convert_fusion.1
  28.1 0.0 all-reduce.7.cloned.1.call-update
  28.1 0.5 reduce-scatter.3.cloned.1.call-start
  28.6 79.6 %all-reduce.7.cloned.1.call-done = (bf16[256,4096]{1,0:T(8,128)(2,1)}, bf16[128,4096]{1,0:T(8,128)(2,1)}) async-done(((bf16[256,4096]{1,0:T(8,128)(2,1)}, bf16[128,4096]{1,0:T(8,128)(2,1)}), (bf16[256,4096]{1,0:T(8,128)(2,1)}, bf16[128,4096]{1,0:T(8,128)(2,1)})) %all-reduce.7.cloned.1.call-update) | async-done | bytes 3145744 | tf_op jit(solution)/shard_map/psum | solution.py:74
  108.2 6.0 fusion.62
  114.2 5.1 bitcast_dynamic-update-slice_fusion.3
  119.3 5.1 bitcast_dynamic-update-slice_fusion.2
  124.4 5.4 convert_dynamic-update-slice_fusion.1
  129.9 1.2 multiply_convert_fusion.1
  131.1 2.4 multiply_convert_fusion.4
  133.6 5.6 bitcast_dynamic-update-slice_fusion.1
  139.1 5.1 bitcast_dynamic-update-slice_fusion
  144.2 5.1 convert_dynamic-update-slice_fusion
  149.3 0.0 all-gather.2.cloned.1.call-start
  149.4 373.3 %reduce-scatter.3.cloned.1.call-done = bf16[1024,5376]{0,1:T(8,128)(2,1)} async-done(((bf16[4096,5376]{0,1:T(8,128)(2,1)}), bf16[1024,5376]{0,1:T(8,128)(2,1)}) %reduce-scatter.3.cloned.1.call-update) | async-done | bytes 11010064 | tf_op jit(solution)/shard_map/reduce_scatter | solution.py:78
  522.7 6.4 convert_element_type.102
  529.1 4.3 multiply_reduce_fusion.1
  533.4 3.3 copy-done
  536.7 39.6 %all-reduce = (f32[]{:T(128)}, f32[]{:T(128)}, f32[]{:T(128)}) all-reduce(f32[]{:T(128)} %get-tuple-element.3, f32[]{:T(128)} %get-tuple-element.4, f32[]{:T(128)} %get-tuple-element.2), channel_id=1, replica_groups=mesh['fsdp'=8,'dp'=4] {'fsdp','dp'}, use_global_device_ids=true, to_apply=%region_8.0 | all-reduce | flops 3 | bytes 24 | tf_op jit(solution)/shard_map/psum | solution.py:92
  578.4 11.2 %add_convert_fusion = bf16[1024,2688]{0,1:T(8,128)(2,1)} fusion(f32[1024,5376]{0,1:T(8,128)} %copy-done, f32[]{:T(128)S(6)} %div.36, f32[]{:T(128)S(6)} %div.35), kind=kLoop, calls=%fused_computation | loop fusion | flops 11010048 | bytes 27525128 | tf_op jit(solution)/shard_map/convert_element_type | solution.py:102
  589.6 0.3 all-reduce.5.cloned.1.call-start
  589.9 202.6 %all-gather.2.cloned.1.call-done = bf16[4096,2688]{0,1:T(8,128)(2,1)} async-done(((bf16[1024,2688]{0,1:T(8,128)(2,1)}), bf16[4096,2688]{0,1:T(8,128)(2,1)}) %all-gather.2.cloned.1.call-update) | async-done | bytes 22020112 | tf_op jit(solution)/shard_map/all_gather | solution.py:103
  792.5 5.6 fusion.27
  798.1 5.8 fusion.30
  804.0 2.6 fusion.47
  806.6 6.8 fusion.21
  813.4 0.0 all-reduce.5.cloned.1.call-update
  813.5 0.3 reduce-scatter.5.cloned.1.call-start
  813.8 64.8 %all-reduce.5.cloned.1.call-done = bf16[256,4096]{1,0:T(8,128)(2,1)} async-done(((bf16[256,4096]{1,0:T(8,128)(2,1)}), bf16[256,4096]{1,0:T(8,128)(2,1)}) %all-reduce.5.cloned.1.call-update) | async-done | bytes 2097168 | tf_op jit(solution)/shard_map/psum | solution.py:111
  878.6 6.2 fusion.61
  884.8 6.6 fusion.33
  891.5 5.1 fusion.48
  896.7 4.0 convolution_add_fusion
  900.6 5.8 fusion.12
  906.4 7.0 fusion.24
  914.1 2.0 multiply_convert_fusion
  916.1 33.0 %reduce-scatter.5.cloned.1.call-done = bf16[256,512]{1,0:T(8,128)(2,1)} async-done(((bf16[256,4096]{1,0:T(8,128)(2,1)}), bf16[256,512]{1,0:T(8,128)(2,1)}) %reduce-scatter.5.cloned.1.call-update) | async-done | bytes 262160 | tf_op jit(solution)/shard_map/reduce_scatter | solution.py:127
  949.1 1.7 multiply_reduce_fusion.3
  950.8 38.0 %psum.55 = f32[]{:T(128)} all-reduce(f32[]{:T(128)} %multiply_reduce_fusion.3), channel_id=1, replica_groups=mesh['fsdp'=8,'dp'=4] {'fsdp','dp'}, use_global_device_ids=true, to_apply=%region_12.0 | all-reduce | flops 1 | bytes 8 | tf_op jit(solution)/shard_map/psum | solution.py:135
  989.4 1.8 fusion.46
  (79 shorter events, 0.2 us)
Async XLA Ops:
  7.2 6.3 copy-start.2
  7.2 101.0 %all-reduce.7.cloned.1.call-start = ((), (), s32[]{:S(2)}) async-start(), calls=%async_computation.6 | async-start | bytes 6291456 | tf_op jit(solution)/shard_map/psum | solution.py:74
  7.2 6.2 copy-start.3
  13.5 1.3 copy-start.13
  13.5 3.4 copy-start.1
  13.5 4.0 copy-start.7
  13.5 8.6 slice-start.2
  17.5 4.6 slice-start.3
  20.8 1.3 copy-start.24
  25.8 82.3 %copy-start.4 = (bf16[128,4096]{1,0:T(8,128)(2,1)S(1)}, bf16[128,4096]{1,0:T(8,128)(2,1)}, u32[]{:S(2)}) copy-start(bf16[128,4096]{1,0:T(8,128)(2,1)} %param.8) | copy-start | bytes 3145732
  28.1 494.6 %reduce-scatter.3.cloned.1.call-start = ((), (), s32[]{:S(2)}) async-start(), calls=%async_computation.2 | async-start | bytes 55050240 | tf_op jit(solution)/shard_map/reduce_scatter | solution.py:78
  119.3 5.2 copy-start.5
  119.3 11.8 %slice-start.4 = ((s8[7340032]{0:T(1024)(128)(4,1)}), s8[4194304]{0:T(1024)(128)(4,1)S(1)}, s32[]{:S(2)}) async-start(s8[7340032]{0:T(1024)(128)(4,1)} %bitcast.48), calls=%async_computation.11 | async-start | bytes 8388608
  124.4 5.4 copy-start.6
  124.4 5.4 copy-start.8
  124.4 5.4 copy-start.12
  124.4 6.6 slice-start.5
  129.8 1.2 copy-start.14
  131.1 13.1 %copy-start.10 = (bf16[256,4096]{1,0:T(8,128)(2,1)}, bf16[256,4096]{1,0:T(8,128)(2,1)S(1)}, u32[]{:S(2)}) copy-start(bf16[256,4096]{1,0:T(8,128)(2,1)S(1)} %multiply_convert_fusion.1) | copy-start | bytes 6291460
  131.1 2.5 copy-start.20
  133.6 5.6 copy-start.15
  139.1 5.1 copy-start.25
  149.3 643.1 %all-gather.2.cloned.1.call-start = ((), (), s32[]{:S(2)}) async-start(), calls=%async_computation.3 | async-start | bytes 27525120 | tf_op jit(solution)/shard_map/all_gather | solution.py:103
  529.1 7.6 copy-start
  578.4 214.1 %copy-start.9 = (bf16[256,4096]{1,0:T(8,128)(2,1)S(1)}, bf16[256,4096]{1,0:T(8,128)(2,1)}, u32[]{:S(2)}) copy-start(bf16[256,4096]{1,0:T(8,128)(2,1)} %param.9) | copy-start | bytes 6291460
  589.6 289.0 %all-reduce.5.cloned.1.call-start = ((), (), s32[]{:S(2)}) async-start(), calls=%async_computation.4 | async-start | bytes 4194304 | tf_op jit(solution)/shard_map/psum | solution.py:111
  792.5 11.4 %slice-start.6 = ((s8[7340032]{0:T(1024)(128)(4,1)}), s8[4194304]{0:T(1024)(128)(4,1)S(1)}, s32[]{:S(2)}) async-start(s8[7340032]{0:T(1024)(128)(4,1)} %bitcast.50), calls=%async_computation.13 | async-start | bytes 8388608
  798.1 5.8 copy-start.18
  798.1 5.9 slice-start.7
  798.1 5.8 copy-start.21
  804.0 2.7 copy-start.23
  804.0 2.7 copy-start.26
  813.4 71.3 %copy-start.11 = (bf16[256,4096]{1,0:T(8,128)(2,1)S(1)}, bf16[256,4096]{1,0:T(8,128)(2,1)}, u32[]{:S(2)}) copy-start(bf16[256,4096]{1,0:T(8,128)(2,1)} %copy-done.10) | copy-start | bytes 6291460
  813.5 135.6 %reduce-scatter.5.cloned.1.call-start = ((), (), s32[]{:S(2)}) async-start(), calls=%async_computation.5 | async-start | bytes 2359296 | tf_op jit(solution)/shard_map/reduce_scatter | solution.py:127
  878.6 12.9 %slice-start.8 = ((s8[7340032]{0:T(1024)(128)(4,1)}), s8[4194304]{0:T(1024)(128)(4,1)S(1)}, s32[]{:S(2)}) async-start(s8[7340032]{0:T(1024)(128)(4,1)} %bitcast.52), calls=%async_computation.15 | async-start | bytes 8388608
  884.8 6.7 slice-start.9
  884.8 6.7 copy-start.16
  884.8 11.8 %slice-start = ((s8[7340032]{0:T(1024)(128)(4,1)}), s8[4194304]{0:T(1024)(128)(4,1)S(1)}, s32[]{:S(2)}) async-start(s8[7340032]{0:T(1024)(128)(4,1)} %bitcast.44), calls=%async_computation.7 | async-start | bytes 8388608
  891.5 5.1 slice-start.1
  891.5 5.1 copy-start.17
  891.5 5.1 copy-start.19
  896.6 4.0 copy-start.22
Sparse Core Ops, SparseCore 0:
  28.2 79.8 all-reduce.6
  149.4 373.1 reduce-scatter.2
  589.7 202.7 all-gather.1
  813.6 64.9 all-reduce.4
  913.5 35.4 reduce-scatter.4
where the time goes:
time: 1010 us; the launch traced here: 999 us
  waiting for transfers between devices  753 us (75%)
  matrix products  113 us (11%)
  blocking collectives  77.6 us (8%)
  other arithmetic  28.6 us (3%)
  between operations  19.3 us (2%)
    reduce_scatter x1, waiting for transfers between devices, local(): lax.psum_scatter(jnp.concatenate([grad_rows(target_x, error_tgt, hidden_t...  373 us
    all_gather x1, waiting for transfers between devices, local(): sens_full = lax.all_gather(local_sens, 'dp', axis=0, tiled=True)  203 us
    psum x1, waiting for transfers between devices, local(): lax.psum(part_poi.astype(jnp.bfloat16), 'fsdp').astype(jnp.float32)  79.6 us
    psum x1, waiting for transfers between devices, local(): lax.psum(part_tan.astype(jnp.bfloat16), 'fsdp').astype(jnp.float32)  64.8 us
    dot_general x8, matrix products, inner_cols(): lax.dot_general(left, right, (((1,), (1,)), ((), ())), preferred_element_...  43.2 us
    psum x1, blocking collectives, local(): lax.psum((jnp.sum(grad_tgt * grad_tgt), jnp.sum(grad_poi * grad_poi), jnp...  39.6 us
    dot_general x10, matrix products, matmul(): return jnp.dot(left, right, preferred_element_type=jnp.float32)  38.7 us
    psum x1, blocking collectives, local(): total_sq = lax.psum(jnp.sum(scaled * scaled), ('fsdp', 'dp'))  38 us
  transfers between devices with their start and end apart: 5, of which 5 were waited for; matrix products, arithmetic and copies ran while one was open for 0% of the time, Pallas kernels for 0%

commit v1 on v0

v1 whole, which is shorter than its diff:
```python
import jax
import jax.numpy as jnp
from jax import lax
from jax.sharding import PartitionSpec as P

EPSILON = 1e-06
BF = jnp.bfloat16
F32 = jnp.float32


def silu_parts(preact):
    sigma = jax.nn.sigmoid(preact)
    silu_val = preact * sigma
    slope = sigma * (1.0 + preact * (1.0 - sigma))
    curve = sigma * (1.0 - sigma) * (2.0 + preact * (1.0 - 2.0 * sigma))
    return (silu_val, slope, curve)


def matmul(left, right):
    return jnp.dot(left, right, preferred_element_type=F32)


def inner_cols(left, right):
    return lax.dot_general(
        left, right, (((1,), (1,)), ((), ())), preferred_element_type=F32
    )


def local(target_x, target_y, poison_x, poison_y, w_gate, w_up, w_down):
    model_width = w_gate.shape[0]
    hidden_width = w_gate.shape[1]
    n_dp = lax.axis_size("dp")
    n_fsdp = lax.axis_size("fsdp")
    n_tgt = target_x.shape[0]
    n_poi = poison_x.shape[0]
    n_row = n_tgt + n_poi
    tgt_total = n_tgt * n_dp
    poi_total = n_poi * n_dp
    columns = model_width // n_fsdp
    first = lax.axis_index("fsdp") * columns

    def own_cols(rows):
        return lax.dynamic_slice_in_dim(rows, first, columns, 1)

    def gather_rows(rows):
        return lax.all_gather(rows, "dp", axis=0, tiled=True)

    is_tgt_loc = jnp.arange(n_row) < n_tgt
    is_tgt_all = (jnp.arange(n_row * n_dp) % n_row) < n_tgt

    rows = jnp.concatenate([target_x, poison_x], axis=0)
    row_cols = own_cols(rows)
    all_cols = gather_rows(row_cols)
    gram_x = lax.psum(inner_cols(row_cols, all_cols).astype(BF), "fsdp")

    gate_pre = matmul(rows, w_gate)
    upper = matmul(rows, w_up)
    silu_val, slope, curve = silu_parts(gate_pre)
    hidden = (silu_val * upper).astype(BF)
    part_out = matmul(hidden, w_down).astype(BF)
    out_cols = lax.psum_scatter(part_out, "fsdp", scatter_dimension=1, tiled=True)
    hidden_all = gather_rows(hidden)
    gram_h_part, gram_x = lax.optimization_barrier(
        (inner_cols(hidden, hidden_all).astype(BF), gram_x)
    )
    gram_h = lax.psum(gram_h_part, "fsdp")

    goal_cols = own_cols(jnp.concatenate([target_y, poison_y], axis=0))
    share = jnp.where(is_tgt_loc, 1.0 / tgt_total, 1.0 / poi_total)[:, None]
    error_cols = (
        (row_cols.astype(F32) + out_cols.astype(F32) - goal_cols.astype(F32)) * share
    ).astype(BF)
    error = lax.all_gather(error_cols, "fsdp", axis=1, tiled=True)
    error_all = gather_rows(error_cols)
    gram_e_part = inner_cols(error_cols, error_all)
    gram_e_own, gram_h = lax.optimization_barrier((gram_e_part[n_tgt:].astype(BF), gram_h))
    gram_e = lax.psum(gram_e_own, "fsdp")
    back = inner_cols(error, w_down)
    back_both = jnp.concatenate([back * upper * slope, back * silu_val], axis=1).astype(BF)
    back_all = gather_rows(back_both)
    gram_b_part = inner_cols(back_both, back_all)
    gram_b_own, gram_e = lax.optimization_barrier((gram_b_part[n_tgt:].astype(BF), gram_e))
    gram_b = lax.psum(gram_b_own, "fsdp")

    both = gram_x.astype(F32) * gram_b_part + gram_h.astype(F32) * gram_e_part
    tgt_cols = jnp.where(is_tgt_all[None, :], both, 0.0)
    sum_tgt = jnp.sum(tgt_cols, axis=1)
    sum_all = jnp.sum(both, axis=1)
    sums = jnp.stack(
        [
            jnp.sum(sum_tgt[:n_tgt]),
            jnp.sum(sum_all[n_tgt:] - sum_tgt[n_tgt:]),
            jnp.sum(sum_tgt[n_tgt:]),
        ]
    )
    sums = lax.psum(sums, ("fsdp", "dp"))
    norm_tt, norm_pp, cross_tp = sums[0], sums[1], sums[2]
    length_tgt = jnp.sqrt(norm_tt + EPSILON)
    length_poi = jnp.sqrt(norm_pp + EPSILON)
    denom = length_tgt * length_poi
    alignment = 1.0 - cross_tp / denom
    coef_tgt = -1.0 / denom
    coef_poi = cross_tp / (denom * length_poi * length_poi)
    coef = jnp.where(is_tgt_all, coef_tgt, coef_poi)[None, :]

    def weigh(gram):
        return (gram.astype(F32) * coef).astype(BF)

    u_poi, s_poi = upper[n_tgt:], silu_val[n_tgt:]
    s1_poi, s2_poi = slope[n_tgt:], curve[n_tgt:]
    b_poi = back[n_tgt:]
    tangents = matmul(weigh(gram_x[n_tgt:]), back_all)
    tan_gate = tangents[:, :hidden_width]
    tan_upper = tangents[:, hidden_width:]
    hidden_tan = (s1_poi * tan_gate * u_poi + s_poi * tan_upper).astype(BF)
    tan_cols = lax.psum_scatter(
        matmul(hidden_tan, w_down).astype(BF), "fsdp", scatter_dimension=1, tiled=True
    ).astype(F32) + matmul(weigh(gram_h[n_tgt:]), error_all)
    back_tan_cols = (tan_cols * (1.0 / poi_total)).astype(BF)
    back_tan = lax.all_gather(back_tan_cols, "fsdp", axis=1, tiled=True)
    mixed = inner_cols(back_tan, w_down) + matmul(weigh(gram_e), hidden_all)
    gate_total = (
        mixed * u_poi * s1_poi + b_poi * (s2_poi * tan_gate * u_poi + s1_poi * tan_upper)
    ).astype(BF)
    upper_total = (mixed * s_poi + b_poi * s1_poi * tan_gate).astype(BF)
    part_grad = inner_cols(gate_total, w_gate) + inner_cols(upper_total, w_up)
    grad_cols = lax.psum_scatter(
        part_grad.astype(BF), "fsdp", scatter_dimension=1, tiled=True
    ).astype(F32)
    grad_cols = grad_cols + matmul(weigh(gram_b), all_cols) + back_tan_cols.astype(F32)
    scaled = grad_cols * float(poi_total * model_width)
    total_sq = lax.psum(jnp.sum(scaled * scaled), ("fsdp", "dp"))
    mean_sq = total_sq / float(poi_total * model_width)
    return (scaled * lax.rsqrt(mean_sq + EPSILON), alignment)


def solution(mesh):
    in_specs = (
        P("dp", None),
        P("dp", None),
        P("dp", None),
        P("dp", None),
        P(None, "fsdp"),
        P(None, "fsdp"),
        P("fsdp", None),
    )
    out_specs = (P("dp", "fsdp"), P())
    return jax.shard_map(local, mesh=mesh, in_specs=in_specs, out_specs=out_specs, check_vma=False)
```

time: 1010 us -> 746 us (0.74)
  waiting for transfers between devices: 753 us -> 552 us
  matrix products: 113 us -> 81.7 us
  other arithmetic: 28.6 us -> 7.48 us
    reduce_scatter x2 -> x3, waiting for transfers between devices: 406 us -> 116 us  [the longest x1 43.1 us: local(): lax.psum_scatter(part_out, 'fsdp', scatter_dimension=1, tiled=True)]
    psum x2 -> x4, waiting for transfers between devices: 144 us -> 211 us  [the longest x1 58.7 us: local(): gram_h = lax.psum(gram_h_part, 'fsdp')]
    dot_general x16 -> x8, matrix products: 70 us -> 38.3 us  [matmul(): return jnp.dot(left, right, preferred_element_type=F32)]
    all_gather x1 -> x6, waiting for transfers between devices: 203 us -> 223 us  [the longest x4 153 us: gather_rows(): return lax.all_gather(rows, 'dp', axis=0, tiled=True)]
    convert_element_type x4 -> x1, other arithmetic: 20.8 us -> 2.16 us  [local(): error_cols = ((row_cols.astype(F32) + out_cols.astype(F32) - goal_cols.as...]
  transfers between devices with their start and end apart: 5 -> 13, of which waited for: 5 -> 13; matrix products, arithmetic and copies ran while one was open for 0% -> 6% of each run, Pallas kernels for 0% -> 0%
where the time goes in v1:
time: 746 us; the launch traced here: 745 us
  waiting for transfers between devices  552 us (74%)
  matrix products  81.7 us (11%)
  blocking collectives  77.2 us (10%)
  between operations  18.9 us (3%)
  other arithmetic  7.48 us (1%)
    all_gather x4, waiting for transfers between devices, gather_rows(): return lax.all_gather(rows, 'dp', axis=0, tiled=True)  153 us
    psum x1, waiting for transfers between devices, local(): gram_h = lax.psum(gram_h_part, 'fsdp')  58.7 us
    psum x1, waiting for transfers between devices, local(): gram_x = lax.psum(inner_cols(row_cols, all_cols).astype(BF), 'fsdp')  57.6 us
    psum x1, waiting for transfers between devices, local(): gram_e = lax.psum(gram_e_own, 'fsdp')  54.8 us
    dot_general x8, matrix products, inner_cols(): lax.dot_general(left, right, (((1,), (1,)), ((), ())), preferred_element_...  43.4 us
    reduce_scatter x1, waiting for transfers between devices, local(): lax.psum_scatter(part_out, 'fsdp', scatter_dimension=1, tiled=True)  43.1 us
    psum x1, waiting for transfers between devices, local(): gram_b = lax.psum(gram_b_own, 'fsdp')  39.8 us
    psum x1, blocking collectives, local(): sums = lax.psum(sums, ('fsdp', 'dp'))  39.3 us
  transfers between devices with their start and end apart: 13, of which 13 were waited for; matrix products, arithmetic and copies ran while one was open for 6% of the time, Pallas kernels for 0%

profile of v1, /device:TPU:0, one launch (start us, length us, event | category | flops | bytes accessed | tf_op | source)
XLA Modules:
  0.0 744.6 jit_solution(8567523727248029789)
XLA Ops:
  7.2 1.4 constant_dynamic-update-slice_fusion.1
  8.7 0.4 copy-done.5
  9.2 6.9 fusion.35
  16.2 5.8 add_divide_fusion
  22.0 8.2 %convolution_convert_fusion = bf16[384,4096]{1,0:T(8,128)(2,1)} fusion(bf16[384,896]{1,0:T(8,128)(2,1)S(1)} %get-tuple-element.23, bf16[896,4096]{1,0:T(8,128)(2,1)} %param.13), kind=kOutput, calls=%fused_computation | convolution fusion | flops 2820145152 | bytes 11173888 | tf_op jit(solution)/shard_map/dot_general | solution.py:20
  30.3 43.1 %reduce-scatter.4.cloned.1.call-done = bf16[384,512]{1,0:T(8,128)(2,1)} async-done(((bf16[384,4096]{1,0:T(8,128)(2,1)}), bf16[384,512]{1,0:T(8,128)(2,1)}) %reduce-scatter.4.cloned.1.call-update) | async-done | bytes 393232 | tf_op jit(solution)/shard_map/reduce_scatter | solution.py:61
  73.5 2.2 multiply_convert_fusion.11
  75.7 0.7 all-gather.7.cloned.1.call-update
  76.4 29.5 %all-gather.9.cloned.1.call-done = bf16[1536,512]{1,0:T(8,128)(2,1)} async-done(((bf16[384,512]{1,0:T(8,128)(2,1)}), bf16[1536,512]{1,0:T(8,128)(2,1)}) %all-gather.9.cloned.1.call-update) | async-done | bytes 1572880 | tf_op jit(solution)/shard_map/all_gather | solution.py:46
  105.9 3.4 convolution_convert_fusion.2
  109.4 0.5 all-gather.11.cloned.1.call-update
  110.0 0.5 all-gather.15.cloned.1.call-update
  110.5 38.0 %all-gather.7.cloned.1.call-done = bf16[1536,896]{1,0:T(8,128)(2,1)} async-done(((bf16[384,896]{1,0:T(8,128)(2,1)}), bf16[1536,896]{1,0:T(8,128)(2,1)}) %all-gather.7.cloned.1.call-update) | async-done | bytes 2752528 | tf_op jit(solution)/shard_map/all_gather | solution.py:46
  148.5 4.3 convolution_convert_fusion.3
  152.8 57.6 %all-reduce.5.cloned.1.call-done = bf16[384,1536]{1,0:T(8,128)(2,1)} async-done(((bf16[384,1536]{1,0:T(8,128)(2,1)}), bf16[384,1536]{1,0:T(8,128)(2,1)}) %all-reduce.5.cloned.1.call-update) | async-done | bytes 1179664 | tf_op jit(solution)/shard_map/psum | solution.py:54
  210.5 39.2 %all-gather.11.cloned.1.call-done = bf16[384,4096]{1,0:T(8,128)(2,1)} async-done(((bf16[384,512]{1,0:T(8,128)(2,1)}), bf16[384,4096]{1,0:T(8,128)(2,1)}) %all-gather.11.cloned.1.call-update) | async-done | bytes 3145744 | tf_op jit(solution)/shard_map/all_gather | solution.py:73
  249.7 9.1 %multiply_convert_fusion.5 = (bf16[384,896]{1,0:T(8,128)(2,1)S(1)}, bf16[384,896]{1,0:T(8,128)(2,1)S(1)}, f32[384,896]{1,0:T(8,128)}) fusion(f32[384,896]{1,0:T(8,128)S(1)} %copy-done.17, f32[384,896]{1,0:T(8,128)} %get-tuple-element.30, bf16[384,4096]{1,0:T(8,128)(2,1)} %all-gather.11.cloned.1.call-done, bf16[896,4096]{1,0:T(8,128)(2,1)} %param.13), kind=kOutput, calls=%fused_computation.18 | convolution fusion | flops 2823045120 | bytes 15990784 | tf_op jit(solution)/shard_map/dot_general | solution.py:24
  258.8 1.2 pad_maximum_fusion
  260.3 21.5 %all-gather.15.cloned.1.call-done = bf16[1536,512]{1,0:T(8,128)(2,1)} async-done(((bf16[384,512]{1,0:T(8,128)(2,1)}), bf16[1536,512]{1,0:T(8,128)(2,1)}) %all-gather.15.cloned.1.call-update) | async-done | bytes 1572880 | tf_op jit(solution)/shard_map/all_gather | solution.py:46
  281.8 2.2 fusion.36
  284.0 1.0 slice.149
  285.0 58.7 %all-reduce.7.cloned.1.call-done = bf16[384,1536]{1,0:T(8,128)(2,1)} async-done(((bf16[384,1536]{1,0:T(8,128)(2,1)}), bf16[384,1536]{1,0:T(8,128)(2,1)}) %all-reduce.7.cloned.1.call-update) | async-done | bytes 1179664 | tf_op jit(solution)/shard_map/psum | solution.py:66
  343.7 64.4 %all-gather.13.cloned.1.call-done = bf16[1536,1792]{1,0:T(8,128)(2,1)} async-done(((bf16[384,1792]{1,0:T(8,128)(2,1)}), bf16[1536,1792]{1,0:T(8,128)(2,1)}) %all-gather.13.cloned.1.call-update) | async-done | bytes 5505040 | tf_op jit(solution)/shard_map/all_gather | solution.py:46
  408.2 7.0 fusion.31
  415.1 0.6 slice_reduce_fusion.1
  415.8 0.6 subtract_reduce_fusion
  416.4 2.0 pad_maximum_fusion.1
  418.4 39.3 %psum.44 = f32[3]{0:T(128)S(1)} all-reduce(f32[3]{0:T(128)S(1)} %pad_maximum_fusion.1), channel_id=1, replica_groups=mesh['fsdp'=8,'dp'=4] {'fsdp','dp'}, use_global_device_ids=true, to_apply=%region_8.9 | all-reduce | flops 3 | bytes 24 | tf_op jit(solution)/shard_map/psum | solution.py:96
  457.7 0.6 fusion.34
  460.4 4.5 fusion.12
  464.9 1.2 copy-done.7
  466.2 6.9 convolution_convert_fusion.1
  473.1 0.5 all-reduce.9.cloned.1.call-update
  473.7 36.0 %reduce-scatter.6.cloned.1.call-done = bf16[256,512]{1,0:T(8,128)(2,1)} async-done(((bf16[256,4096]{1,0:T(8,128)(2,1)}), bf16[256,512]{1,0:T(8,128)(2,1)}) %reduce-scatter.6.cloned.1.call-update) | async-done | bytes 262160 | tf_op jit(solution)/shard_map/reduce_scatter | solution.py:116
  509.7 2.5 fusion.3
  512.3 1.0 slice.148
  513.3 54.8 %all-reduce.9.cloned.1.call-done = bf16[256,1536]{1,0:T(8,128)(2,1)} async-done(((bf16[256,1536]{1,0:T(8,128)(2,1)}), bf16[256,1536]{1,0:T(8,128)(2,1)}) %all-reduce.9.cloned.1.call-update) | async-done | bytes 786448 | tf_op jit(solution)/shard_map/psum | solution.py:77
  568.1 0.3 reduce-scatter.8.cloned.1.call-start
  568.4 30.2 %all-gather.17.cloned.1.call-done = bf16[256,4096]{1,0:T(8,128)(2,1)} async-done(((bf16[256,512]{1,0:T(8,128)(2,1)}), bf16[256,4096]{1,0:T(8,128)(2,1)}) %all-gather.17.cloned.1.call-update) | async-done | bytes 2097168 | tf_op jit(solution)/shard_map/all_gather | solution.py:120
  598.5 6.2 fusion.37
  604.8 1.0 convolution_add_fusion.1
  605.8 7.5 %fusion.19 = f32[256,4096]{1,0:T(8,128)S(1)} fusion(bf16[4096,896]{1,0:T(8,128)(2,1)} %param.11, f32[384,896]{1,0:T(8,128)} %get-tuple-element.24, f32[384,896]{1,0:T(8,128)} %get-tuple-element.30, f32[384,896]{1,0:T(8,128)} %get-tuple-element.22, f32[256,896]{1,0:T(8,128)S(1)} %convolution_add_fusion.1, f32[384,896]{1,0:T(8,128)S(1)} %copy-done.4, ...), kind=kOutput, calls=%fused_computation.50 | convolution fusion | flops 1882488832 | bytes 19791872 | tf_op jit(solution)/shard_map/dot_general | solution.py:24
  613.4 3.8 fusion
  618.0 39.8 %all-reduce.11.cloned.1.call-done = bf16[256,1536]{1,0:T(8,128)(2,1)} async-done(((bf16[256,1536]{1,0:T(8,128)(2,1)}), bf16[256,1536]{1,0:T(8,128)(2,1)}) %all-reduce.11.cloned.1.call-update) | async-done | bytes 786448 | tf_op jit(solution)/shard_map/psum | solution.py:83
  657.8 37.3 %reduce-scatter.8.cloned.1.call-done = bf16[256,512]{1,0:T(8,128)(2,1)} async-done(((bf16[256,4096]{1,0:T(8,128)(2,1)}), bf16[256,512]{1,0:T(8,128)(2,1)}) %reduce-scatter.8.cloned.1.call-update) | async-done | bytes 262160 | tf_op jit(solution)/shard_map/reduce_scatter | solution.py:127
  695.0 2.5 multiply_reduce_fusion
  697.5 37.9 %psum.47 = f32[]{:T(128)} all-reduce(f32[]{:T(128)} %get-tuple-element.33), channel_id=1, replica_groups=mesh['fsdp'=8,'dp'=4] {'fsdp','dp'}, use_global_device_ids=true, to_apply=%region_14.15 | all-reduce | flops 1 | bytes 8 | tf_op jit(solution)/shard_map/psum | solution.py:132
  736.1 0.8 broadcast_multiply_fusion
  (83 shorter events, 1.1 us)
Async XLA Ops:
  7.2 1.9 copy-start.5
  7.2 66.3 %reduce-scatter.4.cloned.1.call-start = ((), (), s32[]{:S(2)}) async-start(), calls=%async_computation.6 | async-start | bytes 3538944 | tf_op jit(solution)/shard_map/reduce_scatter | solution.py:61
  9.1 7.1 slice-start
  9.2 7.0 copy-start.15
  9.2 7.0 slice-start.1
  16.2 5.8 copy-start.16
  22.0 8.2 %copy-start.13 = (bf16[384,896]{1,0:T(8,128)(2,1)}, bf16[384,896]{1,0:T(8,128)(2,1)S(1)}, u32[]{:S(2)}) copy-start(bf16[384,896]{1,0:T(8,128)(2,1)S(1)} %get-tuple-element.23) | copy-start | bytes 2064388
  30.2 43.2 %copy-start.6 = (bf16[256,4096]{1,0:T(8,128)(2,1)S(1)}, bf16[256,4096]{1,0:T(8,128)(2,1)}, u32[]{:S(2)}) copy-start(bf16[256,4096]{1,0:T(8,128)(2,1)} %param.10) | copy-start | bytes 6291460
  30.2 43.2 %copy-start.10 = (bf16[128,4096]{1,0:T(8,128)(2,1)S(1)}, bf16[128,4096]{1,0:T(8,128)(2,1)}, u32[]{:S(2)}) copy-start(bf16[128,4096]{1,0:T(8,128)(2,1)} %param.8) | copy-start | bytes 3145732
  30.3 75.6 %all-gather.9.cloned.1.call-start = ((), (), s32[]{:S(2)}) async-start(), calls=%async_computation.4 | async-start | bytes 1966080 | tf_op jit(solution)/shard_map/all_gather | solution.py:46
  75.7 72.9 %all-gather.7.cloned.1.call-start = ((), (), s32[]{:S(2)}) async-start(), calls=%async_computation.3 | async-start | bytes 3440640 | tf_op jit(solution)/shard_map/all_gather | solution.py:46
  76.4 134.0 %all-reduce.5.cloned.1.call-start = ((), (), s32[]{:S(2)}) async-start(), calls=%async_computation.5 | async-start | bytes 2359296 | tf_op jit(solution)/shard_map/psum | solution.py:54
  109.3 39.2 %copy-start.14 = (bf16[384,896]{1,0:T(8,128)(2,1)S(1)}, bf16[384,896]{1,0:T(8,128)(2,1)}, u32[]{:S(2)}) copy-start(bf16[384,896]{1,0:T(8,128)(2,1)} %copy-done.13) | copy-start | bytes 2064388
  109.3 140.4 %all-gather.11.cloned.1.call-start = ((), (), s32[]{:S(2)}) async-start(), calls=%async_computation.7 | async-start | bytes 3538944 | tf_op jit(solution)/shard_map/all_gather | solution.py:73
  109.9 171.9 %all-gather.15.cloned.1.call-start = ((), (), s32[]{:S(2)}) async-start(), calls=%async_computation.9 | async-start | bytes 1966080 | tf_op jit(solution)/shard_map/all_gather | solution.py:46
  110.5 139.2 %copy-start.17 = (f32[384,896]{1,0:T(8,128)S(1)}, f32[384,896]{1,0:T(8,128)}, u32[]{:S(2)}) copy-start(f32[384,896]{1,0:T(8,128)} %copy-done.16) | copy-start | bytes 4128772
  110.5 233.2 %all-reduce.7.cloned.1.call-start = ((), (), s32[]{:S(2)}) async-start(), calls=%async_computation.10 | async-start | bytes 2359296 | tf_op jit(solution)/shard_map/psum | solution.py:66
  210.4 197.8 %all-gather.13.cloned.1.call-start = ((), (), s32[]{:S(2)}) async-start(), calls=%async_computation.8 | async-start | bytes 6881280 | tf_op jit(solution)/shard_map/all_gather | solution.py:46
  258.8 1.3 copy-start.12
  258.8 23.0 %copy-start = (bf16[384,512]{1,0:T(8,128)(2,1)S(1)}, bf16[384,512]{1,0:T(8,128)(2,1)}, u32[]{:S(2)}) copy-start(bf16[384,512]{1,0:T(8,128)(2,1)} %get-tuple-element.18) | copy-start | bytes 1179652
  260.1 249.6 %reduce-scatter.6.cloned.1.call-start = ((), (), s32[]{:S(2)}) async-start(), calls=%async_computation.11 | async-start | bytes 2359296 | tf_op jit(solution)/shard_map/reduce_scatter | solution.py:116
  460.4 5.8 copy-start.2
  460.4 5.8 copy-start.18
  460.4 5.8 copy-start.20
  464.9 1.2 copy-start.7
  473.1 36.7 %copy-start.9 = (bf16[1536,512]{1,0:T(8,128)(2,1)S(1)}, bf16[1536,512]{1,0:T(8,128)(2,1)}, u32[]{:S(2)}) copy-start(bf16[1536,512]{1,0:T(8,128)(2,1)} %all-gather.15.cloned.1.call-done) | copy-start | bytes 4718596
  473.1 95.0 %all-reduce.9.cloned.1.call-start = ((), (), s32[]{:S(2)}) async-start(), calls=%async_computation.13 | async-start | bytes 1572864 | tf_op jit(solution)/shard_map/psum | solution.py:77
  473.7 38.6 %copy-start.22 = (bf16[384,1536]{1,0:T(8,128)(2,1)S(1)}, bf16[384,1536]{1,0:T(8,128)(2,1)}, u32[]{:S(2)}) copy-start(bf16[384,1536]{1,0:T(8,128)(2,1)} %get-tuple-element.32) | copy-start | bytes 3538948
  473.7 124.8 %all-gather.17.cloned.1.call-start = ((), (), s32[]{:S(2)}) async-start(), calls=%async_computation.12 | async-start | bytes 2359296 | tf_op jit(solution)/shard_map/all_gather | solution.py:120
  512.2 145.5 %all-reduce.11.cloned.1.call-start = ((), (), s32[]{:S(2)}) async-start(), calls=%async_computation.15 | async-start | bytes 1572864 | tf_op jit(solution)/shard_map/psum | solution.py:83
  568.1 36.7 %copy-start.1 = (bf16[1536,896]{1,0:T(8,128)(2,1)S(1)}, bf16[1536,896]{1,0:T(8,128)(2,1)}, u32[]{:S(2)}) copy-start(bf16[1536,896]{1,0:T(8,128)(2,1)} %all-gather.7.cloned.1.call-done) | copy-start | bytes 8257540
  568.1 36.7 %copy-start.11 = (bf16[256,1536]{1,0:T(8,128)(2,1)S(1)}, bf16[256,1536]{1,0:T(8,128)(2,1)}, u32[]{:S(2)}) copy-start(bf16[256,1536]{1,0:T(8,128)(2,1)} %all-reduce.9.cloned.1.call-done) | copy-start | bytes 2359300
  568.1 126.9 %reduce-scatter.8.cloned.1.call-start = ((), (), s32[]{:S(2)}) async-start(), calls=%async_computation.14 | async-start | bytes 2359296 | tf_op jit(solution)/shard_map/reduce_scatter | solution.py:127
  598.5 7.3 copy-start.3
  598.5 7.3 copy-start.4
  598.5 7.3 copy-start.19
  604.8 8.6 %slice-start.2 = ((s8[7340032]{0:T(1024)(128)(4,1)}), s8[4194304]{0:T(1024)(128)(4,1)S(1)}, s32[]{:S(2)}) async-start(s8[7340032]{0:T(1024)(128)(4,1)} %bitcast.32), calls=%async_computation.18 | async-start | bytes 8388608
  605.8 7.6 %slice-start.3 = ((s8[7340032]{0:T(1024)(128)(4,1)}), s8[3145728]{0:T(1024)(128)(4,1)S(1)}, s32[]{:S(2)}) async-start(s8[7340032]{0:T(1024)(128)(4,1)} %bitcast.32), calls=%async_computation.19 | async-start | bytes 6291456
  605.8 7.6 %copy-start.8 = (f32[256,1792]{1,0:T(8,128)S(1)}, f32[256,1792]{1,0:T(8,128)}, u32[]{:S(2)}) copy-start(f32[256,1792]{1,0:T(8,128)} %copy-done.7) | copy-start | bytes 5505028
  605.8 7.6 %copy-start.21 = (f32[384,896]{1,0:T(8,128)S(1)}, f32[384,896]{1,0:T(8,128)}, u32[]{:S(2)}) copy-start(f32[384,896]{1,0:T(8,128)} %get-tuple-element.25) | copy-start | bytes 4128772
  617.2 77.8 %copy-start.23 = (bf16[256,512]{1,0:T(8,128)(2,1)S(1)}, bf16[256,512]{1,0:T(8,128)(2,1)}, u32[]{:S(2)}) copy-start(bf16[256,512]{1,0:T(8,128)(2,1)} %fusion.3) | copy-start | bytes 786436
  617.2 77.8 %copy-start.24 = (bf16[1536,512]{1,0:T(8,128)(2,1)S(1)}, bf16[1536,512]{1,0:T(8,128)(2,1)}, u32[]{:S(2)}) copy-start(bf16[1536,512]{1,0:T(8,128)(2,1)} %all-gather.9.cloned.1.call-done) | copy-start | bytes 4718596
Sparse Core Ops, SparseCore 0:
  30.4 43.0 reduce-scatter.3
  75.8 30.0 all-gather.8
  107.8 40.7 all-gather.6
  150.7 59.6 all-reduce.4
  212.4 37.2 all-gather.10
  252.0 29.8 all-gather.14
  284.2 59.4 all-reduce.6
  345.6 62.5 all-gather.12
  473.2 36.4 reduce-scatter.5
  511.9 56.0 all-reduce.8
  570.3 28.1 all-gather.16
  600.8 56.8 all-reduce.10
  660.1 34.9 reduce-scatter.7

commit v2 on v1

v2 whole, which is shorter than its diff:
```python
import functools
import jax
import jax.numpy as jnp
from jax import lax
from jax.experimental import pallas as pl
from jax.experimental.pallas import tpu as pltpu
from jax.sharding import PartitionSpec as P

EPSILON = 1e-06
BF = jnp.bfloat16
F32 = jnp.float32

MESH = pl.DeviceIdType.MESH
STEP = 16


def columns_of(width):
    return lambda ref, i: ref.at[:, pl.ds(pl.multiple_of(i * width, width), width)]


def rows_of(height):
    return lambda ref, i: ref.at[pl.ds(pl.multiple_of(i * height, height), height)]


def over_rows(count, body, init=0):
    return lax.fori_loop(
        0, count // STEP, lambda i, c: body(pl.ds(pl.multiple_of(i * STEP, STEP), STEP), i, c), init
    )


class Exchange:
    def __init__(self, n_fsdp, n_dp, send, recv, local_sem):
        self.n, self.n_dp, self.groups = n_fsdp, n_dp, n_fsdp // 2
        self.send, self.recv, self.local_sem = send, recv, local_sem
        self.count, self.local_count = 0, 0
        self.open, self.local_open = [], []
        self.me = lax.axis_index("fsdp")
        self.row = lax.axis_index("dp")
        self.core = lax.rem(self.me, 2)
        self.group = lax.div(self.me, 2)
        self.twin = {"fsdp": 2 * self.group + 1 - self.core}

    def ahead(self, k):
        return lax.rem(self.group + k, self.groups)

    def behind(self, k):
        return lax.rem(self.group + self.groups - k, self.groups)

    def peer(self, k):
        return {"fsdp": 2 * self.ahead(k) + self.core}

    def dp_peer(self, k):
        return {"dp": lax.rem(self.row + k, self.n_dp)}

    def greet(self, fsdp, dp, every=False):
        targets = []
        if every:
            targets += [{"fsdp": lax.rem(self.me + k, self.n)} for k in range(1, self.n)]
        elif fsdp:
            targets += [self.twin] + [self.peer(k) for k in range(1, self.groups)]
        if dp:
            targets += [self.dp_peer(k) for k in range(1, self.n_dp)]
        barrier = pltpu.get_barrier_semaphore()
        for device in targets:
            pl.semaphore_signal(barrier, inc=1, device_id=device, device_id_type=MESH)
        pl.semaphore_wait(barrier, len(targets))

    def start(self, src, dst, device):
        copy = pltpu.make_async_remote_copy(
            src_ref=src,
            dst_ref=dst,
            send_sem=self.send.at[self.count],
            recv_sem=self.recv.at[self.count],
            device_id=device,
            device_id_type=MESH,
        )
        copy.start()
        self.count += 1
        self.open.append(copy)
        return copy

    def keep(self, src, dst):
        copy = pltpu.make_async_copy(src, dst, self.local_sem.at[self.local_count])
        copy.start()
        self.local_count += 1
        self.local_open.append(copy)

    def finish(self):
        for copy in self.open:
            copy.wait_send()
        for copy in self.local_open:
            copy.wait()

    def dp_gather(self, src, dst):
        height = src.shape[0]
        own = dst.at[pl.ds(pl.multiple_of(self.row * height, height), height)]
        self.keep(src, own)
        return [self.start(src, own, self.dp_peer(k)) for k in range(1, self.n_dp)]

    def reduce_open(self, part, piece, twin_buf):
        order = list(range(1, self.groups)) + [0]
        return {
            k: self.start(
                piece(part, 2 * self.ahead(k) + 1 - self.core), twin_buf.at[k], self.twin
            )
            for k in order
        }

    def reduce_send(self, part, piece, twin_buf, half, far_buf, opened):
        sent = []
        for k in range(1, self.groups):
            mine = piece(part, 2 * self.ahead(k) + self.core)
            opened[k].wait_recv()

            def add(rows, i, c, mine=mine, k=k):
                half[k - 1, rows, :] = (
                    mine[rows, :].astype(F32) + twin_buf[k, rows, :].astype(F32)
                ).astype(BF)
                return c

            over_rows(half.shape[1], add)
            sent.append(self.start(half.at[k - 1], far_buf.at[k - 1], self.peer(k)))
        return sent

    def reduce_close(self, part, piece, twin_buf, far_buf, opened, sent):
        opened[0].wait_recv()
        for copy in sent:
            copy.wait_recv()
        mine = piece(part, self.me)

        def total(rows):
            value = mine[rows, :].astype(F32) + twin_buf[0, rows, :].astype(F32)
            for k in range(1, self.groups):
                value = value + far_buf[k - 1, rows, :].astype(F32)
            return value

        return total

    def spread_open(self, own, full, piece):
        target = piece(full, self.me)
        self.keep(own, target)
        far = [self.start(own, target, self.peer(k)) for k in range(1, self.groups)]
        return far, [self.start(own, target, self.twin)]

    def spread_close(self, full, piece, far, near):
        for k in range(1, self.groups):
            far[k - 1].wait_recv()
            block = piece(full, 2 * self.behind(k) + self.core)
            near.append(self.start(block, block, self.twin))
        for copy in near:
            copy.wait_recv()

    def sum_tiles(self, tiles, row_tiles):
        copies = [
            self.start(
                tiles.at[self.me], tiles.at[self.me], {"fsdp": lax.rem(self.me + k, self.n)}
            )
            for k in range(1, self.n)
        ]
        for copy in copies:
            copy.wait_recv()
        value = tiles[0]
        for j in range(1, self.n):
            value = value + tiles[j]
        row_tiles[self.row] = value
        copies = [
            self.start(row_tiles.at[self.row], row_tiles.at[self.row], self.dp_peer(k))
            for k in range(1, self.n_dp)
        ]
        for copy in copies:
            copy.wait_recv()
        value = row_tiles[0]
        for j in range(1, self.n_dp):
            value = value + row_tiles[j]
        return value


def reduce_scratch(n, height, width):
    g = n // 2
    return [
        pltpu.VMEM((g, height, width), BF),
        pltpu.VMEM((g - 1, height, width), BF),
        pltpu.VMEM((g - 1, height, width), BF),
    ]


def communicate(body, n, n_dp, copies, kept, outs, ins, scratch, ident, flops=0):
    sems = [
        pltpu.SemaphoreType.DMA((copies,)),
        pltpu.SemaphoreType.DMA((copies,)),
        pltpu.SemaphoreType.DMA((max(kept, 1),)),
    ]

    def kernel(*refs):
        ex = Exchange(n, n_dp, refs[-3], refs[-2], refs[-1])
        body(ex, *refs[:-3])
        ex.finish()
        assert ex.count == copies and ex.local_count == kept, (ex.count, ex.local_count)

    vmem = pl.BlockSpec(memory_space=pltpu.VMEM)
    anyw = pl.BlockSpec(memory_space=pl.ANY)
    return pl.pallas_call(
        kernel,
        out_shape=[jax.ShapeDtypeStruct(shape, kind) for shape, kind, _ in outs],
        in_specs=[vmem if v else anyw for _, v in ins],
        out_specs=[vmem if v else anyw for _, _, v in outs],
        scratch_shapes=list(scratch) + sems,
        compiler_params=pltpu.CompilerParams(
            collective_id=ident, has_side_effects=True, vmem_limit_bytes=40 * 1024 * 1024
        ),
    )(*[a for a, _ in ins])


def forward_exchange(n, n_dp, n_tgt, part, row_cols, goal_cols, hidden):
    height, width = row_cols.shape
    piece = columns_of(width)
    tgt_share, poi_share = 1.0 / (n_tgt * n_dp), 1.0 / ((height - n_tgt) * n_dp)

    def body(ex, part, x, goal, hidden, error, own, all_x, all_h, all_e, twin, half, far):
        ex.greet(True, True)
        opened = ex.reduce_open(part, piece, twin)
        gathers = ex.dp_gather(x, all_x) + ex.dp_gather(hidden, all_h)
        sent = ex.reduce_send(part, piece, twin, half, far, opened)
        total = ex.reduce_close(part, piece, twin, far, opened, sent)

        def loss(rows, i, c):
            share = jnp.where(i * STEP < n_tgt, tgt_share, poi_share)
            value = x[rows, :].astype(F32) + total(rows) - goal[rows, :].astype(F32)
            own[rows, :] = (value * share).astype(BF)
            return c

        over_rows(height, loss)
        spread = ex.spread_open(own, error, piece)
        gathers += ex.dp_gather(own, all_e)
        ex.spread_close(error, piece, *spread)
        for copy in gathers:
            copy.wait_recv()

    g = n // 2
    return communicate(
        body, n, n_dp, g + (g - 1) + (g - 1) + g + 3 * (n_dp - 1), 4,
        [
            ((height, width * n), BF, True),
            ((height, width), BF, True),
            ((height * n_dp, width), BF, False),
            ((height * n_dp, hidden.shape[1]), BF, False),
            ((height * n_dp, width), BF, False),
        ],
        [(part, True), (row_cols, True), (goal_cols, True), (hidden, False)],
        reduce_scratch(n, height, width), 1,
    )


def gram_exchange(n, n_dp, grams, back_both):
    height, width = grams.shape
    piece = rows_of(height // n)

    def body(ex, grams, back, summed, all_b, own, twin, half, far):
        ex.greet(True, True)
        opened = ex.reduce_open(grams, piece, twin)
        gathers = ex.dp_gather(back, all_b)
        sent = ex.reduce_send(grams, piece, twin, half, far, opened)
        total = ex.reduce_close(grams, piece, twin, far, opened, sent)

        def store(rows, i, c):
            own[rows, :] = total(rows).astype(BF)
            return c

        over_rows(height // n, store)
        ex.spread_close(summed, piece, *ex.spread_open(own, summed, piece))
        for copy in gathers:
            copy.wait_recv()

    g = n // 2
    return communicate(
        body, n, n_dp, g + (g - 1) + (g - 1) + g + (n_dp - 1), 2,
        [
            ((height, width), BF, True),
            ((back_both.shape[0] * n_dp, back_both.shape[1]), BF, False),
        ],
        [(grams, True), (back_both, False)],
        [pltpu.VMEM((height // n, width), BF)] + reduce_scratch(n, height // n, width), 2,
    )


def sum_exchange(n, n_dp, tile):
    def body(ex, tile, out, tiles, row_tiles):
        ex.greet(True, True, every=True)
        tiles[ex.me] = tile[...]
        out[...] = ex.sum_tiles(tiles, row_tiles)

    return communicate(
        body, n, n_dp, (n - 1) + (n_dp - 1), 0,
        [(tile.shape, F32, True)],
        [(tile, True)],
        [pltpu.VMEM((n,) + tile.shape, F32), pltpu.VMEM((n_dp,) + tile.shape, F32)], 3,
    )[0]


def tangent_exchange(n, n_dp, poi_total, part, extra, gram):
    height, width = extra.shape
    piece = columns_of(width)
    low = gram.shape[0] // n
    low_piece = rows_of(low)

    def body(ex, part, extra, gram, full, own, summed, low_own, t1, h1, f1, t2, h2, f2):
        ex.greet(True, False)
        opened = ex.reduce_open(part, piece, t1)
        low_opened = ex.reduce_open(gram, low_piece, t2)
        sent = ex.reduce_send(part, piece, t1, h1, f1, opened)
        low_sent = ex.reduce_send(gram, low_piece, t2, h2, f2, low_opened)
        total = ex.reduce_close(part, piece, t1, f1, opened, sent)

        def store(rows, i, c):
            own[rows, :] = ((total(rows) + extra[rows, :]) * (1.0 / poi_total)).astype(BF)
            return c

        over_rows(height, store)
        spread = ex.spread_open(own, full, piece)
        low_total = ex.reduce_close(gram, low_piece, t2, f2, low_opened, low_sent)

        def low_store(rows, i, c):
            low_own[rows, :] = low_total(rows).astype(BF)
            return c

        over_rows(low, low_store)
        low_spread = ex.spread_open(low_own, summed, low_piece)
        ex.spread_close(full, piece, *spread)
        ex.spread_close(summed, low_piece, *low_spread)

    g = n // 2
    return communicate(
        body, n, n_dp, 2 * (g + (g - 1) + (g - 1) + g), 2,
        [((height, width * n), BF, True), ((height, width), BF, True), (gram.shape, BF, True)],
        [(part, True), (extra, True), (gram, True)],
        [pltpu.VMEM((low, gram.shape[1]), BF)]
        + reduce_scratch(n, height, width)
        + reduce_scratch(n, low, gram.shape[1]), 4,
    )


def final_exchange(n, n_dp, scale, entries, part, extra):
    height, width = extra.shape
    piece = columns_of(width)

    def body(ex, part, extra, out, twin, half, far, tiles, row_tiles):
        ex.greet(True, True, every=True)
        opened = ex.reduce_open(part, piece, twin)
        sent = ex.reduce_send(part, piece, twin, half, far, opened)
        total = ex.reduce_close(part, piece, twin, far, opened, sent)

        def store(rows, i, c):
            value = (total(rows) + extra[rows, :]) * scale
            out[rows, :] = value
            return c + value * value

        squares = over_rows(height, store, jnp.zeros((STEP, width), F32))
        tiles[ex.me] = jnp.broadcast_to(jnp.sum(squares), (8, 128))
        summed = ex.sum_tiles(tiles, row_tiles)
        factor = lax.rsqrt(jnp.max(summed) / entries + EPSILON)

        def rescale(rows, i, c):
            out[rows, :] = out[rows, :] * factor
            return c

        over_rows(height, rescale)

    g = n // 2
    return communicate(
        body, n, n_dp, g + (g - 1) + (n - 1) + (n_dp - 1), 0,
        [((height, width), F32, True)],
        [(part, True), (extra, True)],
        reduce_scratch(n, height, width)
        + [pltpu.VMEM((n, 8, 128), F32), pltpu.VMEM((n_dp, 8, 128), F32)], 5,
    )[0]


def silu_parts(preact):
    sigma = jax.nn.sigmoid(preact)
    silu_val = preact * sigma
    slope = sigma * (1.0 + preact * (1.0 - sigma))
    curve = sigma * (1.0 - sigma) * (2.0 + preact * (1.0 - 2.0 * sigma))
    return (silu_val, slope, curve)


def matmul(left, right):
    return jnp.dot(left, right, preferred_element_type=F32)


def inner_cols(left, right):
    return lax.dot_general(
        left, right, (((1,), (1,)), ((), ())), preferred_element_type=F32
    )


def local(target_x, target_y, poison_x, poison_y, w_gate, w_up, w_down):
    model_width = w_gate.shape[0]
    hidden_width = w_gate.shape[1]
    n_dp = lax.axis_size("dp")
    n_fsdp = lax.axis_size("fsdp")
    n_tgt = target_x.shape[0]
    n_poi = poison_x.shape[0]
    n_row = n_tgt + n_poi
    tgt_total = n_tgt * n_dp
    poi_total = n_poi * n_dp
    columns = model_width // n_fsdp
    first = lax.axis_index("fsdp") * columns

    def own_cols(rows):
        return lax.dynamic_slice_in_dim(rows, first, columns, 1)

    is_tgt_all = (jnp.arange(n_row * n_dp) % n_row) < n_tgt

    rows = jnp.concatenate([target_x, poison_x], axis=0)
    row_cols = own_cols(rows)
    goal_cols = jnp.concatenate([own_cols(target_y), own_cols(poison_y)], axis=0)

    gate_pre = matmul(rows, w_gate)
    upper = matmul(rows, w_up)
    silu_val, slope, curve = silu_parts(gate_pre)
    hidden = (silu_val * upper).astype(BF)
    part_out = matmul(hidden, w_down).astype(BF)
    error, error_cols, all_cols, hidden_all, error_all = forward_exchange(
        n_fsdp, n_dp, n_tgt, part_out, row_cols, goal_cols, hidden
    )

    back = inner_cols(error, w_down)
    back_both = jnp.concatenate([back * upper * slope, back * silu_val], axis=1).astype(BF)
    gram_e_part = inner_cols(error_cols, error_all)
    grams, back_all = gram_exchange(
        n_fsdp,
        n_dp,
        jnp.concatenate(
            [
                inner_cols(row_cols, all_cols).astype(BF),
                inner_cols(hidden, hidden_all).astype(BF),
                gram_e_part[n_tgt:].astype(BF),
            ],
            axis=0,
        ),
        back_both,
    )
    gram_x, gram_h, gram_e = grams[:n_row], grams[n_row : 2 * n_row], grams[2 * n_row :]
    gram_b_part = inner_cols(back_both, back_all)

    both = gram_x.astype(F32) * gram_b_part + gram_h.astype(F32) * gram_e_part
    sum_tgt = jnp.sum(jnp.where(is_tgt_all[None, :], both, 0.0), axis=1)
    sum_poi = jnp.sum(jnp.where(is_tgt_all[None, :], 0.0, both), axis=1)
    sums = jnp.stack(
        [jnp.sum(sum_tgt[:n_tgt]), jnp.sum(sum_poi[n_tgt:]), jnp.sum(sum_tgt[n_tgt:])]
    )
    tile = jnp.broadcast_to(jnp.pad(sums, (0, 5))[:, None], (8, 128))
    sums = sum_exchange(n_fsdp, n_dp, tile)[:, 0]
    norm_tt, norm_pp, cross_tp = sums[0], sums[1], sums[2]
    length_tgt = jnp.sqrt(norm_tt + EPSILON)
    length_poi = jnp.sqrt(norm_pp + EPSILON)
    denom = length_tgt * length_poi
    alignment = 1.0 - cross_tp / denom
    coef_tgt = -1.0 / denom
    coef_poi = cross_tp / (denom * length_poi * length_poi)
    coef = jnp.where(is_tgt_all, coef_tgt, coef_poi)[None, :]

    def weigh(gram):
        return (gram.astype(F32) * coef).astype(BF)

    u_poi, s_poi = upper[n_tgt:], silu_val[n_tgt:]
    s1_poi, s2_poi = slope[n_tgt:], curve[n_tgt:]
    b_poi = back[n_tgt:]
    tangents = matmul(weigh(gram_x[n_tgt:]), back_all)
    tan_gate = tangents[:, :hidden_width]
    tan_upper = tangents[:, hidden_width:]
    hidden_tan = (s1_poi * tan_gate * u_poi + s_poi * tan_upper).astype(BF)
    back_tan, back_tan_cols, gram_b = tangent_exchange(
        n_fsdp,
        n_dp,
        poi_total,
        matmul(hidden_tan, w_down).astype(BF),
        matmul(weigh(gram_h[n_tgt:]), error_all),
        gram_b_part[n_tgt:].astype(BF),
    )
    mixed = inner_cols(back_tan, w_down) + matmul(weigh(gram_e), hidden_all)
    gate_total = (
        mixed * u_poi * s1_poi + b_poi * (s2_poi * tan_gate * u_poi + s1_poi * tan_upper)
    ).astype(BF)
    upper_total = (mixed * s_poi + b_poi * s1_poi * tan_gate).astype(BF)
    part_grad = inner_cols(gate_total, w_gate) + inner_cols(upper_total, w_up)
    step = final_exchange(
        n_fsdp,
        n_dp,
        float(poi_total * model_width),
        float(poi_total * model_width),
        part_grad.astype(BF),
        matmul(weigh(gram_b), all_cols) + back_tan_cols.astype(F32),
    )
    return (step, alignment)


def solution(mesh):
    in_specs = (
        P("dp", None),
        P("dp", None),
        P("dp", None),
        P("dp", None),
        P(None, "fsdp"),
        P(None, "fsdp"),
        P("fsdp", None),
    )
    out_specs = (P("dp", "fsdp"), P())
    return jax.shard_map(local, mesh=mesh, in_specs=in_specs, out_specs=out_specs, check_vma=False)
```

time: 746 us -> 352 us (0.47)
  waiting for transfers between devices: 552 us -> 0 us
  Pallas kernels: 0 us -> 273 us
  blocking collectives: 77.2 us -> 0 us
  matrix products: 81.7 us -> 59.9 us
  between operations: 18.9 us -> 4.97 us
    pallas_call x0 -> x5, Pallas kernels: none -> 273 us  [communicate(): pl.pallas_call(kernel, out_shape=[jax.ShapeDtypeStruct(shape, kind) for s...]
    all_gather x6 -> x0, waiting for transfers between devices: 223 us -> none  [the longest x4 153 us: gather_rows(): return lax.all_gather(rows, 'dp', axis=0, tiled=True)]
    psum x4 -> x0, waiting for transfers between devices: 211 us -> none  [the longest x1 58.7 us: local(): gram_h = lax.psum(gram_h_part, 'fsdp')]
    reduce_scatter x3 -> x0, waiting for transfers between devices: 116 us -> none  [the longest x1 43.1 us: local(): lax.psum_scatter(part_out, 'fsdp', scatter_dimension=1, tiled=True)]
    psum x2 -> x0, blocking collectives: 77.2 us -> none  [the longest x1 39.3 us: local(): sums = lax.psum(sums, ('fsdp', 'dp'))]
    dot_general x8, matrix products: 38.3 us -> 27.3 us  [matmul(): return jnp.dot(left, right, preferred_element_type=F32)]
    dot_general x8, matrix products: 43.4 us -> 32.6 us  [inner_cols(): lax.dot_general(left, right, (((1,), (1,)), ((), ())), preferred_element_...]
  transfers between devices with their start and end apart: 13 -> 0, of which waited for: 13 -> 0; matrix products, arithmetic and copies ran while one was open for 6% -> 0% of each run, Pallas kernels for 0% -> 0%
where the time goes in v2:
time: 352 us
  Pallas kernels  273 us (78%)
  matrix products  59.9 us (17%)
  local copies, waits for them, and re-layouts  9.72 us (3%)
  between operations  4.97 us (1%)
  other arithmetic  4.32 us (1%)
    pallas_call x5, Pallas kernels, communicate(): pl.pallas_call(kernel, out_shape=[jax.ShapeDtypeStruct(shape, kind) for s...  273 us
    dot_general x8, matrix products, inner_cols(): lax.dot_general(left, right, (((1,), (1,)), ((), ())), preferred_element_...  32.6 us
    dot_general x8, matrix products, matmul(): return jnp.dot(left, right, preferred_element_type=F32)  27.3 us

profile of v2, /device:TPU:0, one launch (start us, length us, event | category | flops | bytes accessed | tf_op | source)
XLA Modules:
  0.0 352.1 jit_solution(5134078332468713178)
XLA Ops:
  0.6 0.0 copy-start
  0.7 1.6 copy-done
  2.2 0.9 constant_dynamic-slice_fusion.1
  3.2 0.0 copy-start.8
  3.2 1.5 constant_dynamic-update-slice_fusion.1
  4.7 2.1 constant_dynamic-update-slice_fusion
  6.7 0.0 slice-start
  6.7 0.1 pad_maximum_fusion.2
  6.8 0.4 copy-done.8
  7.2 3.4 fusion.31
  10.6 5.9 %add_multiply_fusion = (f32[384,896]{1,0:T(8,128)}, bf16[384,896]{1,0:T(8,128)(2,1)S(1)}, f32[384,896]{1,0:T(8,128)}, f32[384,896]{1,0:T(8,128)}, f32[384,896]{1,0:T(8,128)}, /*index=5*/f32[384,896]{1,0:T(8,128)S(1)}) fusion(f32[384,896]{1,0:T(8,128)S(1)} %fusion.31, bf16[384,4096]{1,0:T(8,128)(2,1)S(1)} %constant_dynamic-update-slice_fusion, ...), kind=kOutput, calls=%fused_computation.20 | convolution fusion | flops 2822012928 | bytes 19431424 | tf_op jit(solution)/shard_map/dot_general | solution.py:387
  16.5 7.2 %convolution_convert_fusion.refs_0_ = bf16[384,4096]{1,0:T(8,128)(2,1)S(1)} fusion(bf16[384,896]{1,0:T(8,128)(2,1)S(1)} %get-tuple-element.27.refs_3_, bf16[896,4096]{1,0:T(8,128)(2,1)} %param.13), kind=kOutput, calls=%fused_computation | convolution fusion | flops 2820145152 | bytes 11173888 | tf_op jit(solution)/shard_map/dot_general | solution.py:387
  23.8 71.1 %shard_map.86 = (bf16[384,4096]{1,0:T(8,128)(2,1)S(1)}, bf16[384,512]{1,0:T(8,128)(2,1)S(1)}, bf16[1536,512]{1,0:T(8,128)(2,1)S(1)}, bf16[1536,896]{1,0:T(8,128)(2,1)S(1)}, bf16[1536,512]{1,0:T(8,128)(2,1)S(1)}) custom-call(bf16[384,4096]{1,0:T(8,128)(2,1)S(1)} %convolution_convert_fusion.refs_0_, bf16[384,512]{1,0:T(8,128)(2,1)S(1)} %get-tuple-element.38.refs_1_, ...), custom_call_target="tpu_custom_call" | custom-call | tf_op jit(solution)/shard_map/pallas_call | solution.py:202
  94.9 8.9 %multiply_convert_fusion.5 = (bf16[384,896]{1,0:T(8,128)(2,1)S(1)}, bf16[384,896]{1,0:T(8,128)(2,1)S(1)}, f32[384,896]{1,0:T(8,128)}) fusion(f32[384,896]{1,0:T(8,128)S(1)} %fusion.31, f32[384,896]{1,0:T(8,128)S(1)} %get-tuple-element.34, bf16[384,4096]{1,0:T(8,128)(2,1)S(1)} %get-tuple-element.16, bf16[896,4096]{1,0:T(8,128)(2,1)} %param.13), kind=kOutput, calls=%fused_computation.18 | convolution fusion | flops 2823045120 | bytes 15990784 | tf_op jit(solution)/shard_map/dot_general | solution.py:391
  103.8 0.1 pad_maximum_fusion.1.refs_1_
  104.0 0.8 convolution_convert_fusion.3
  104.8 0.8 fusion.32
  105.6 0.1 slice.182
  105.7 1.4 convolution_convert_fusion.2
  107.1 0.3 pad_maximum_fusion.refs_0_
  107.4 78.2 %shard_map.87 = (bf16[1024,1536]{1,0:T(8,128)(2,1)S(1)}, bf16[1536,1792]{1,0:T(8,128)(2,1)S(1)}) custom-call(bf16[1024,1536]{1,0:T(8,128)(2,1)S(1)} %pad_maximum_fusion.refs_0_, bf16[384,1792]{1,0:T(8,128)(2,1)S(1)} %pad_maximum_fusion.1.refs_1_), custom_call_target="tpu_custom_call" | custom-call | tf_op jit(solution)/shard_map/pallas_call | solution.py:202
  185.6 3.7 %select_reduce_fusion = (f32[384]{0:T(512)S(1)}, f32[384]{0:T(512)S(1)}, bf16[384,1536]{1,0:T(8,128)(2,1)}) fusion(pred[1536]{0:T(1024)(128)(4,1)S(1)} %fusion.22, f32[384,1536]{1,0:T(8,128)S(1)} %fusion.32, bf16[1024,1536]{1,0:T(8,128)(2,1)S(1)} %get-tuple-element.17, bf16[1536,1792]{1,0:T(8,128)(2,1)S(1)} %get-tuple-element.18, ...), kind=kOutput, calls=%fused_computation.7 | convolution fusion | flops 2122579200 | bytes 12784128 | tf_op jit(solution)/shard_map/dot_general | solution.py:391
  189.4 0.7 slice_reduce_fusion.2
  190.0 0.6 slice_reduce_fusion.1
  190.6 0.6 slice_reduce_fusion
  191.2 2.0 select_maximum_fusion
  193.2 0.1 broadcast_in_dim.41.refs_0_
  193.3 19.2 %shard_map.88 = f32[8,128]{1,0:T(8,128)S(1)} custom-call(f32[8,128]{1,0:T(8,128)S(1)} %broadcast_in_dim.41.refs_0_), custom_call_target="tpu_custom_call" | custom-call | tf_op jit(solution)/shard_map/pallas_call | solution.py:202
  212.6 0.6 fusion.30
  215.9 0.0 slice-start.4
  215.9 2.4 fusion.10.refs_1_
  218.3 0.2 copy-done.4
  218.5 4.4 %fusion.9 = f32[256,1792]{1,0:T(8,128)S(1)} fusion(bf16[1536,1792]{1,0:T(8,128)(2,1)} %copy-done.5, f32[1536]{0:T(1024)S(1)} %broadcast_select_fusion, bf16[1024,1536]{1,0:T(8,128)(2,1)S(1)} %copy-done.4), kind=kOutput, calls=%fused_computation.36 | convolution fusion | flops 1410465792 | bytes 8134656 | tf_op jit(solution)/shard_map/dot_general | solution.py:387
  223.0 0.7 slice-done.5
  223.7 2.5 convolution_convert_fusion.1.refs_0_
  226.1 0.1 slice.181.refs_2_
  226.2 66.8 %shard_map.89 = (bf16[256,4096]{1,0:T(8,128)(2,1)S(1)}, bf16[256,512]{1,0:T(8,128)(2,1)S(1)}, bf16[256,1536]{1,0:T(8,128)(2,1)S(1)}) custom-call(bf16[256,4096]{1,0:T(8,128)(2,1)S(1)} %convolution_convert_fusion.1.refs_0_, f32[256,512]{1,0:T(8,128)S(1)} %fusion.10.refs_1_, bf16[256,1536]{1,0:T(8,128)(2,1)S(1)} %slice.181.refs_2_), custom_call_target="tpu_custom_call" | custom-call | tf_op jit(solution)/shard_map/pallas_call | solution.py:202
  293.0 0.6 convolution_add_fusion.2.refs_1_
  293.6 0.0 slice-start.2
  293.6 5.6 %fusion.33 = f32[256,896]{1,0:T(8,128)S(1)} fusion(bf16[256,4096]{1,0:T(8,128)(2,1)S(1)} %get-tuple-element.19, bf16[896,4096]{1,0:T(8,128)(2,1)} %param.13), kind=kOutput, calls=%fused_computation.75 | convolution fusion | flops 1879048192 | bytes 10354688 | tf_op jit(solution)/shard_map/dot_general | solution.py:391
  299.3 1.0 convolution_add_fusion.1
  300.3 0.3 copy-done.10
  300.6 0.4 copy-done.14
  301.0 5.0 %fusion.18 = f32[256,4096]{1,0:T(8,128)S(1)} fusion(bf16[4096,896]{1,0:T(8,128)(2,1)S(1)} %bitcast.33, f32[384,896]{1,0:T(8,128)} %get-tuple-element.28, f32[384,896]{1,0:T(8,128)} %copy-done.16, f32[384,896]{1,0:T(8,128)} %get-tuple-element.30, f32[256,896]{1,0:T(8,128)S(1)} %convolution_add_fusion.1, f32[384,896]{1,0:T(8,128)S(1)} %copy-done.10, ...), kind=kOutput, calls=%fused_computation.46 | convolution fusion | flops 1882488832 | bytes 19791872 | tf_op jit(solution)/shard_map/dot_general | solution.py:391
  306.0 0.0 copy-start.1
  306.0 6.3 %fusion.refs_0_ = bf16[256,4096]{1,0:T(8,128)(2,1)S(1)} fusion(f32[256,4096]{1,0:T(8,128)S(1)} %fusion.18, bf16[4096,896]{1,0:T(8,128)(2,1)} %param.12, f32[256,896]{1,0:T(8,128)S(1)} %convolution_add_fusion.1, f32[384,896]{1,0:T(8,128)S(1)} %copy-done.10, f32[384,896]{1,0:T(8,128)} %get-tuple-element.29, f32[256,1792]{1,0:T(8,128)} %copy-done.11, ...), kind=kOutput, calls=%fused_computation.3 | convolution fusion | flops 1882292224 | bytes 18219008 | tf_op jit(solution)/shard_map/dot_general | solution.py:391
  312.4 37.8 %shard_map.90 = f32[256,512]{1,0:T(8,128)S(1)} custom-call(bf16[256,4096]{1,0:T(8,128)(2,1)S(1)} %fusion.refs_0_, f32[256,512]{1,0:T(8,128)S(1)} %convolution_add_fusion.2.refs_1_), custom_call_target="tpu_custom_call" | custom-call | tf_op jit(solution)/shard_map/pallas_call | solution.py:202
  350.2 0.8 copy.11
  (42 shorter events, 0.1 us)
Async XLA Ops:
  0.6 1.6 copy-start
  3.2 4.0 %copy-start.8 = (bf16[4096,896]{1,0:T(8,128)(2,1)S(1)}, bf16[4096,896]{1,0:T(8,128)(2,1)}, u32[]{:S(2)}) copy-start(bf16[4096,896]{1,0:T(8,128)(2,1)} %param.12) | copy-start | bytes 22020100
  6.7 3.9 %slice-start = ((s8[7340032]{0:T(1024)(128)(4,1)}), s8[4194304]{0:T(1024)(128)(4,1)S(1)}, s32[]{:S(2)}) async-start(s8[7340032]{0:T(1024)(128)(4,1)} %bitcast.30), calls=%async_computation | async-start | bytes 8388608
  7.2 3.4 slice-start.1
  10.6 84.3 %copy-start.12 = (f32[384,896]{1,0:T(8,128)}, f32[384,896]{1,0:T(8,128)S(1)}, u32[]{:S(2)}) copy-start(f32[384,896]{1,0:T(8,128)S(1)} %fusion.31) | copy-start | bytes 4128772
  16.5 78.4 %copy-start.16 = (f32[384,896]{1,0:T(8,128)}, f32[384,896]{1,0:T(8,128)S(1)}, u32[]{:S(2)}) copy-start(f32[384,896]{1,0:T(8,128)S(1)} %get-tuple-element.34) | copy-start | bytes 4128772
  94.9 9.1 %copy-start.6 = (bf16[1536,512]{1,0:T(8,128)(2,1)}, bf16[1536,512]{1,0:T(8,128)(2,1)S(1)}, u32[]{:S(2)}) copy-start(bf16[1536,512]{1,0:T(8,128)(2,1)S(1)} %get-tuple-element.12) | copy-start | bytes 4718596
  94.9 9.9 %copy-start.2 = (bf16[1536,512]{1,0:T(8,128)(2,1)}, bf16[1536,512]{1,0:T(8,128)(2,1)S(1)}, u32[]{:S(2)}) copy-start(bf16[1536,512]{1,0:T(8,128)(2,1)S(1)} %get-tuple-element.15) | copy-start | bytes 4718596
  185.6 3.8 %copy-start.3 = (bf16[1024,1536]{1,0:T(8,128)(2,1)}, bf16[1024,1536]{1,0:T(8,128)(2,1)S(1)}, u32[]{:S(2)}) copy-start(bf16[1024,1536]{1,0:T(8,128)(2,1)S(1)} %get-tuple-element.17) | copy-start | bytes 9437188
  185.6 3.8 %copy-start.5 = (bf16[1536,1792]{1,0:T(8,128)(2,1)}, bf16[1536,1792]{1,0:T(8,128)(2,1)S(1)}, u32[]{:S(2)}) copy-start(bf16[1536,1792]{1,0:T(8,128)(2,1)S(1)} %get-tuple-element.18) | copy-start | bytes 16515076
  215.9 2.6 copy-start.4
  215.9 7.0 %slice-start.4 = ((s8[7340032]{0:T(1024)(128)(4,1)}), s8[4194304]{0:T(1024)(128)(4,1)S(1)}, s32[]{:S(2)}) async-start(s8[7340032]{0:T(1024)(128)(4,1)} %bitcast.34), calls=%async_computation.4 | async-start | bytes 8388608
  218.5 4.5 %copy-start.9 = (f32[384,896]{1,0:T(8,128)S(1)}, f32[384,896]{1,0:T(8,128)}, u32[]{:S(2)}) copy-start(f32[384,896]{1,0:T(8,128)} %get-tuple-element.26) | copy-start | bytes 4128772
  218.5 4.5 %copy-start.13 = (f32[384,896]{1,0:T(8,128)S(1)}, f32[384,896]{1,0:T(8,128)}, u32[]{:S(2)}) copy-start(f32[384,896]{1,0:T(8,128)} %copy-done.12) | copy-start | bytes 4128772
  218.5 4.5 %copy-start.15 = (f32[384,896]{1,0:T(8,128)S(1)}, f32[384,896]{1,0:T(8,128)}, u32[]{:S(2)}) copy-start(f32[384,896]{1,0:T(8,128)} %get-tuple-element.29) | copy-start | bytes 4128772
  218.5 5.2 %slice-start.5 = ((s8[7340032]{0:T(1024)(128)(4,1)}), s8[3145728]{0:T(1024)(128)(4,1)S(1)}, s32[]{:S(2)}) async-start(s8[7340032]{0:T(1024)(128)(4,1)} %bitcast.34), calls=%async_computation.5 | async-start | bytes 6291456
  222.9 3.2 copy-start.11
  223.7 2.5 copy-start.17
  226.2 66.8 %copy-start.7 = (bf16[1536,512]{1,0:T(8,128)(2,1)S(1)}, bf16[1536,512]{1,0:T(8,128)(2,1)}, u32[]{:S(2)}) copy-start(bf16[1536,512]{1,0:T(8,128)(2,1)} %copy-done.6) | copy-start | bytes 4718596
  293.6 6.6 %slice-start.2 = ((s8[7340032]{0:T(1024)(128)(4,1)}), s8[4194304]{0:T(1024)(128)(4,1)S(1)}, s32[]{:S(2)}) async-start(s8[7340032]{0:T(1024)(128)(4,1)} %bitcast.32), calls=%async_computation.2 | async-start | bytes 8388608
  293.6 6.6 %slice-start.3 = ((s8[7340032]{0:T(1024)(128)(4,1)}), s8[3145728]{0:T(1024)(128)(4,1)S(1)}, s32[]{:S(2)}) async-start(s8[7340032]{0:T(1024)(128)(4,1)} %bitcast.32), calls=%async_computation.3 | async-start | bytes 6291456
  299.2 1.3 copy-start.10
  299.2 1.7 copy-start.14
  306.0 45.0 %copy-start.1 = (bf16[256,4096]{1,0:T(8,128)(2,1)S(1)}, bf16[256,4096]{1,0:T(8,128)(2,1)}, u32[]{:S(2)}) copy-start(bf16[256,4096]{1,0:T(8,128)(2,1)} %param.10) | copy-start | bytes 6291460

commit v3 on v2

--- a/solution.py
+++ b/solution.py
@@ -39,15 +39,8 @@
         self.core = lax.rem(self.me, 2)
         self.group = lax.div(self.me, 2)
         self.twin = {"fsdp": 2 * self.group + 1 - self.core}
-
-    def ahead(self, k):
-        return lax.rem(self.group + k, self.groups)
-
-    def behind(self, k):
-        return lax.rem(self.group + self.groups - k, self.groups)
-
-    def peer(self, k):
-        return {"fsdp": 2 * self.ahead(k) + self.core}
+        self.above = {"fsdp": lax.rem(self.me + 2, self.n)}
+        self.below = {"fsdp": lax.rem(self.me + self.n - 2, self.n)}
 
     def dp_peer(self, k):
         return {"dp": lax.rem(self.row + k, self.n_dp)}
@@ -57,7 +50,8 @@
         if every:
             targets += [{"fsdp": lax.rem(self.me + k, self.n)} for k in range(1, self.n)]
         elif fsdp:
-            targets += [self.twin] + [self.peer(k) for k in range(1, self.groups)]
+            targets += [self.twin]
+            targets += [{"fsdp": lax.rem(self.me + 2 * k, self.n)} for k in range(1, self.groups)]
         if dp:
             targets += [self.dp_peer(k) for k in range(1, self.n_dp)]
         barrier = pltpu.get_barrier_semaphore()
@@ -65,7 +59,7 @@
             pl.semaphore_signal(barrier, inc=1, device_id=device, device_id_type=MESH)
         pl.semaphore_wait(barrier, len(targets))
 
-    def start(self, src, dst, device):
+    def plan(self, src, dst, device, when=None):
         copy = pltpu.make_async_remote_copy(
             src_ref=src,
             dst_ref=dst,
@@ -74,9 +68,13 @@
             device_id=device,
             device_id_type=MESH,
         )
+        self.count += 1
+        self.open.append((copy, when))
+        return copy
+
+    def start(self, src, dst, device):
+        copy = self.plan(src, dst, device)
         copy.start()
-        self.count += 1
-        self.open.append(copy)
         return copy
 
     def keep(self, src, dst):
@@ -86,69 +84,174 @@
         self.local_open.append(copy)
 
     def finish(self):
-        for copy in self.open:
-            copy.wait_send()
+        for copy, when in self.open:
+            if when is None:
+                copy.wait_send()
+            else:
+                pl.when(when)(copy.wait_send)
         for copy in self.local_open:
             copy.wait()
 
     def dp_gather(self, src, dst):
         height = src.shape[0]
-        own = dst.at[pl.ds(pl.multiple_of(self.row * height, height), height)]
+        place = lambda i, at, size: dst.at[pl.ds(pl.multiple_of(i * height + at, STEP), size)]
+        own = place(self.row, 0, height)
         self.keep(src, own)
-        return [self.start(src, own, self.dp_peer(k)) for k in range(1, self.n_dp)]
+        if self.n_dp != 4:
+            return [self.start(src, own, self.dp_peer(k)) for k in range(1, self.n_dp)], []
+        across = self.row + 1 - 2 * lax.rem(self.row, 2)
+        along = lax.rem(self.row + 2, 4)
+        first = self.start(src, own, {"dp": across})
+        second = self.start(src, own, {"dp": along})
+        size = height // 2
+        upper, lower = place(across, 0, size), place(along, size, size)
+        return [], [
+            (first, self.plan(upper, upper, {"dp": along})),
+            (second, self.plan(lower, lower, {"dp": across})),
+        ]
+
+    def dp_forward(self, gather):
+        direct, pairs = gather
+        for arrived, onward in pairs:
+            arrived.wait_recv()
+            onward.start()
+
+    def dp_close(self, gather):
+        direct, pairs = gather
+        for copy in direct + [onward for _, onward in pairs]:
+            copy.wait_recv()
 
     def reduce_open(self, part, piece, twin_buf):
-        order = list(range(1, self.groups)) + [0]
+        order = []
+        for k in range((self.groups + 1) // 2):
+            order += [self.groups - 1 - k] + ([k] if k != self.groups - 1 - k else [])
         return {
-            k: self.start(
-                piece(part, 2 * self.ahead(k) + 1 - self.core), twin_buf.at[k], self.twin
+            d: self.start(piece(part, 2 * d + 1 - self.core), twin_buf.at[d], self.twin)
+            for d in order
+        }
+
+    def reduce_send(self, part, piece, twin_buf, half, far_buf, opened):
+        g, last = self.group, self.groups - 1
+        ups, downs = [], []
+        for s in range(last):
+            ups.append(self.plan(half.at[0, s], far_buf.at[0, s], self.above, g < last - s))
+            downs.append(self.plan(half.at[1, s], far_buf.at[1, s], self.below, g > s))
+
+        def hop(way, s):
+            target = last - s if way == 0 else s
+            copy = (ups if way == 0 else downs)[s]
+            inner = g > 0 if way == 0 else g < last
+            mine = piece(part, 2 * target + self.core)
+
+            def add(with_far):
+                def step(rows, i, c):
+                    value = mine[rows, :].astype(F32) + twin_buf[target, rows, :].astype(F32)
+                    if with_far:
+                        value = value + far_buf[way, s, rows, :].astype(F32)
+                    half[way, s, rows, :] = value.astype(BF)
+                    return c
+
+                over_rows(half.shape[2], step)
+
+            @pl.when(g < target if way == 0 else g > target)
+            def _():
+                opened[target].wait_recv()
+
+                @pl.when(inner)
+                def _():
+                    copy.wait_recv()
+                    add(True)
+
+                @pl.when(jnp.logical_not(inner))
+                def _():
+                    add(False)
+
+                copy.start()
+
+        @pl.when(g < self.groups // 2)
+        def _():
+            for s in range(last):
+                hop(0, s)
+                hop(1, s)
+
+        @pl.when(g >= self.groups // 2)
+        def _():
+            for s in range(last):
+                hop(1, s)
+                hop(0, s)
+
+        return ups, downs
+
+    def reduce_close(self, part, piece, twin_buf, half, far_buf, opened, sent):
+        g, last = self.group, self.groups - 1
+        ups, downs = sent
+        for d in range(self.groups):
+            pl.when(g == d)(opened[d].wait_recv)
+        for s in range(last):
+            pl.when(jnp.logical_and(g == last - s, g > 0))(ups[s].wait_recv)
+            pl.when(jnp.logical_and(g == s, g < last))(downs[s].wait_recv)
+        mine = piece(part, self.me)
+        from_below = jnp.clip(last - g, 0, last - 1)
+        from_above = jnp.clip(g, 0, last - 1)
+
+        def apply(store, height, init=0):
+            def run(below, above):
+                def step(rows, i, c):
+                    value = mine[rows, :].astype(F32) + twin_buf[g, rows, :].astype(F32)
+                    if below:
+                        value = value + far_buf[0, from_below, rows, :].astype(F32)
+                    if above:
+                        value = value + far_buf[1, from_above, rows, :].astype(F32)
+                    return store(value, rows, i, c)
+
+                return over_rows(height, step, init)
+
+            return lax.cond(
+                g == 0,
+                lambda: run(False, True),
+                lambda: lax.cond(g == last, lambda: run(True, False), lambda: run(True, True)),
             )
-            for k in order
-        }
-
-    def reduce_send(self, part, piece, twin_buf, half, far_buf, opened):
-        sent = []
-        for k in range(1, self.groups):
-            mine = piece(part, 2 * self.ahead(k) + self.core)
-            opened[k].wait_recv()
-
-            def add(rows, i, c, mine=mine, k=k):
-                half[k - 1, rows, :] = (
-                    mine[rows, :].astype(F32) + twin_buf[k, rows, :].astype(F32)
-                ).astype(BF)
-                return c
-
-            over_rows(half.shape[1], add)
-            sent.append(self.start(half.at[k - 1], far_buf.at[k - 1], self.peer(k)))
-        return sent
-
-    def reduce_close(self, part, piece, twin_buf, far_buf, opened, sent):
-        opened[0].wait_recv()
-        for copy in sent:
-            copy.wait_recv()
-        mine = piece(part, self.me)
-
-        def total(rows):
-            value = mine[rows, :].astype(F32) + twin_buf[0, rows, :].astype(F32)
-            for k in range(1, self.groups):
-                value = value + far_buf[k - 1, rows, :].astype(F32)
-            return value
-
-        return total
-
-    def spread_open(self, own, full, piece):
+
+        return apply
+
+    def spread(self, own, full, piece, between=None):
+        g, last = self.group, self.groups - 1
         target = piece(full, self.me)
         self.keep(own, target)
-        far = [self.start(own, target, self.peer(k)) for k in range(1, self.groups)]
-        return far, [self.start(own, target, self.twin)]
-
-    def spread_close(self, full, piece, far, near):
-        for k in range(1, self.groups):
-            far[k - 1].wait_recv()
-            block = piece(full, 2 * self.behind(k) + self.core)
-            near.append(self.start(block, block, self.twin))
-        for copy in near:
-            copy.wait_recv()
+        near = [(self.start(own, target, self.twin), None)]
+        hops = []
+        for t in range(last):
+            for way, device in ((1, self.above), (-1, self.below)):
+                block = own if t == 0 else piece(full, 2 * ((g - way * t + self.groups) % self.groups) + self.core)
+                there = target if t == 0 else block
+                sends = jnp.logical_and(g < last, g >= t) if way == 1 else jnp.logical_and(g > 0, g + t <= last)
+                gets = g >= t + 1 if way == 1 else g + t + 1 <= last
+                come = piece(full, 2 * ((g - way * (t + 1) + self.groups) % self.groups) + self.core)
+                hops.append((t, self.plan(block, there, device, sends), sends, gets,
+                             self.plan(come, come, self.twin, gets)))
+        for t in range(last):
+            mine = [hop for hop in hops if hop[0] == t]
+            for _, copy, sends, _, _ in mine:
+                pl.when(sends)(copy.start)
+            if t == 0 and between is not None:
+                between()
+            for _, copy, _, gets, onward in mine:
+
+                def pass_on(copy=copy, onward=onward):
+                    copy.wait_recv()
+                    onward.start()
+
+                pl.when(gets)(pass_on)
+                near.append((onward, gets))
+
+        def close():
+            for copy, gets in near:
+                if gets is None:
+                    copy.wait_recv()
+                else:
+                    pl.when(gets)(copy.wait_recv)
+
+        return close
 
     def sum_tiles(self, tiles, row_tiles):
         copies = [
@@ -179,8 +282,8 @@
     g = n // 2
     return [
         pltpu.VMEM((g, height, width), BF),
-        pltpu.VMEM((g - 1, height, width), BF),
-        pltpu.VMEM((g - 1, height, width), BF),
+        pltpu.VMEM((2, g - 1, height, width), BF),
+        pltpu.VMEM((2, g - 1, height, width), BF),
     ]
 
 
@@ -195,7 +298,7 @@
         ex = Exchange(n, n_dp, refs[-3], refs[-2], refs[-1])
         body(ex, *refs[:-3])
         ex.finish()
-        assert ex.count == copies and ex.local_count == kept, (ex.count, ex.local_count)
+        assert ex.count <= copies and ex.local_count == kept, (ex.count, ex.local_count)
 
     vmem = pl.BlockSpec(memory_space=pltpu.VMEM)
     anyw = pl.BlockSpec(memory_space=pl.ANY)
@@ -219,26 +322,31 @@
     def body(ex, part, x, goal, hidden, error, own, all_x, all_h, all_e, twin, half, far):
         ex.greet(True, True)
         opened = ex.reduce_open(part, piece, twin)
-        gathers = ex.dp_gather(x, all_x) + ex.dp_gather(hidden, all_h)
+        gathers = [ex.dp_gather(x, all_x), ex.dp_gather(hidden, all_h)]
         sent = ex.reduce_send(part, piece, twin, half, far, opened)
-        total = ex.reduce_close(part, piece, twin, far, opened, sent)
-
-        def loss(rows, i, c):
+        apply = ex.reduce_close(part, piece, twin, half, far, opened, sent)
+
+        def loss(total, rows, i, c):
             share = jnp.where(i * STEP < n_tgt, tgt_share, poi_share)
-            value = x[rows, :].astype(F32) + total(rows) - goal[rows, :].astype(F32)
+            value = x[rows, :].astype(F32) + total - goal[rows, :].astype(F32)
             own[rows, :] = (value * share).astype(BF)
             return c
 
-        over_rows(height, loss)
-        spread = ex.spread_open(own, error, piece)
-        gathers += ex.dp_gather(own, all_e)
-        ex.spread_close(error, piece, *spread)
-        for copy in gathers:
-            copy.wait_recv()
-
-    g = n // 2
+        apply(loss, height)
+
+        def between():
+            for gather in gathers:
+                ex.dp_forward(gather)
+            gathers.append(ex.dp_gather(own, all_e))
+
+        close = ex.spread(own, error, piece, between)
+        ex.dp_forward(gathers[-1])
+        close()
+        for gather in gathers:
+            ex.dp_close(gather)
+
     return communicate(
-        body, n, n_dp, g + (g - 1) + (g - 1) + g + 3 * (n_dp - 1), 4,
+        body, n, n_dp, 6 * n + 3 * n_dp, 4,
         [
             ((height, width * n), BF, True),
             ((height, width), BF, True),
@@ -258,22 +366,21 @@
     def body(ex, grams, back, summed, all_b, own, twin, half, far):
         ex.greet(True, True)
         opened = ex.reduce_open(grams, piece, twin)
-        gathers = ex.dp_gather(back, all_b)
+        gather = ex.dp_gather(back, all_b)
         sent = ex.reduce_send(grams, piece, twin, half, far, opened)
-        total = ex.reduce_close(grams, piece, twin, far, opened, sent)
-
-        def store(rows, i, c):
-            own[rows, :] = total(rows).astype(BF)
+        apply = ex.reduce_close(grams, piece, twin, half, far, opened, sent)
+
+        def store(total, rows, i, c):
+            own[rows, :] = total.astype(BF)
             return c
 
-        over_rows(height // n, store)
-        ex.spread_close(summed, piece, *ex.spread_open(own, summed, piece))
-        for copy in gathers:
-            copy.wait_recv()
-
-    g = n // 2
+        apply(store, height // n)
+        close = ex.spread(own, summed, piece, lambda: ex.dp_forward(gather))
+        close()
+        ex.dp_close(gather)
+
     return communicate(
-        body, n, n_dp, g + (g - 1) + (g - 1) + g + (n_dp - 1), 2,
+        body, n, n_dp, 6 * n + n_dp, 2,
         [
             ((height, width), BF, True),
             ((back_both.shape[0] * n_dp, back_both.shape[1]), BF, False),
@@ -309,28 +416,27 @@
         low_opened = ex.reduce_open(gram, low_piece, t2)
         sent = ex.reduce_send(part, piece, t1, h1, f1, opened)
         low_sent = ex.reduce_send(gram, low_piece, t2, h2, f2, low_opened)
-        total = ex.reduce_close(part, piece, t1, f1, opened, sent)
-
-        def store(rows, i, c):
-            own[rows, :] = ((total(rows) + extra[rows, :]) * (1.0 / poi_total)).astype(BF)
+        apply = ex.reduce_close(part, piece, t1, h1, f1, opened, sent)
+
+        def store(total, rows, i, c):
+            own[rows, :] = ((total + extra[rows, :]) * (1.0 / poi_total)).astype(BF)
             return c
 
-        over_rows(height, store)
-        spread = ex.spread_open(own, full, piece)
-        low_total = ex.reduce_close(gram, low_piece, t2, f2, low_opened, low_sent)
-
-        def low_store(rows, i, c):
-            low_own[rows, :] = low_total(rows).astype(BF)
+        apply(store, height)
+        close = ex.spread(own, full, piece)
+        low_apply = ex.reduce_close(gram, low_piece, t2, h2, f2, low_opened, low_sent)
+
+        def low_store(total, rows, i, c):
+            low_own[rows, :] = total.astype(BF)
             return c
 
-        over_rows(low, low_store)
-        low_spread = ex.spread_open(low_own, summed, low_piece)
-        ex.spread_close(full, piece, *spread)
-        ex.spread_close(summed, low_piece, *low_spread)
-
-    g = n // 2
+        low_apply(low_store, low)
+        low_close = ex.spread(low_own, summed, low_piece)
+        close()
+        low_close()
+
     return communicate(
-        body, n, n_dp, 2 * (g + (g - 1) + (g - 1) + g), 2,
+        body, n, n_dp, 12 * n, 2,
         [((height, width * n), BF, True), ((height, width), BF, True), (gram.shape, BF, True)],
         [(part, True), (extra, True), (gram, True)],
         [pltpu.VMEM((low, gram.shape[1]), BF)]
@@ -347,14 +453,14 @@
         ex.greet(True, True, every=True)
         opened = ex.reduce_open(part, piece, twin)
         sent = ex.reduce_send(part, piece, twin, half, far, opened)
-        total = ex.reduce_close(part, piece, twin, far, opened, sent)
-
-        def store(rows, i, c):
-            value = (total(rows) + extra[rows, :]) * scale
+        apply = ex.reduce_close(part, piece, twin, half, far, opened, sent)
+
+        def store(total, rows, i, c):
+            value = (total + extra[rows, :]) * scale
             out[rows, :] = value
             return c + value * value
 
-        squares = over_rows(height, store, jnp.zeros((STEP, width), F32))
+        squares = apply(store, height, jnp.zeros((STEP, width), F32))
         tiles[ex.me] = jnp.broadcast_to(jnp.sum(squares), (8, 128))
         summed = ex.sum_tiles(tiles, row_tiles)
         factor = lax.rsqrt(jnp.max(summed) / entries + EPSILON)
@@ -365,9 +471,8 @@
 
         over_rows(height, rescale)
 
-    g = n // 2
     return communicate(
-        body, n, n_dp, g + (g - 1) + (n - 1) + (n_dp - 1), 0,
+        body, n, n_dp, 4 * n + n_dp, 0,
         [((height, width), F32, True)],
         [(part, True), (extra, True)],
         reduce_scratch(n, height, width)

time: 352 us -> 329 us (0.935)
  Pallas kernels: 273 us -> 250 us
    pallas_call x5, Pallas kernels: 273 us -> 250 us  [communicate(): pl.pallas_call(kernel, out_shape=[jax.ShapeDtypeStruct(shape, kind) for s...]
where the time goes in v3:
time: 329 us
  Pallas kernels  250 us (76%)
  matrix products  59.7 us (18%)
  local copies, waits for them, and re-layouts  9.74 us (3%)
  between operations  4.97 us (2%)
  other arithmetic  4.32 us (1%)
    pallas_call x5, Pallas kernels, communicate(): pl.pallas_call(kernel, out_shape=[jax.ShapeDtypeStruct(shape, kind) for s...  250 us
    dot_general x8, matrix products, inner_cols(): lax.dot_general(left, right, (((1,), (1,)), ((), ())), preferred_element_...  32.6 us
    dot_general x8, matrix products, matmul(): return jnp.dot(left, right, preferred_element_type=F32)  27.1 us

profile of v3, /device:TPU:0, one launch (start us, length us, event | category | flops | bytes accessed | tf_op | source)
XLA Modules:
  0.0 328.9 jit_solution(17558236971857506082)
XLA Ops:
  0.6 0.0 copy-start
  0.7 1.6 copy-done
  2.2 0.9 constant_dynamic-slice_fusion.1
  3.2 0.0 copy-start.8
  3.2 1.5 constant_dynamic-update-slice_fusion.1
  4.7 2.1 constant_dynamic-update-slice_fusion
  6.7 0.0 slice-start
  6.7 0.1 pad_maximum_fusion.2
  6.8 0.4 copy-done.8
  7.2 3.4 %fusion.31 = f32[384,896]{1,0:T(8,128)S(1)} fusion(bf16[384,4096]{1,0:T(8,128)(2,1)S(1)} %constant_dynamic-update-slice_fusion, bf16[4096,896]{1,0:T(8,128)(2,1)S(1)} %copy-done.8), kind=kOutput, calls=%fused_computation.73 | convolution fusion | flops 2818572288 | bytes 11862016 | tf_op jit(solution)/shard_map/dot_general | solution.py:492
  10.6 5.7 %add_multiply_fusion = (f32[384,896]{1,0:T(8,128)}, bf16[384,896]{1,0:T(8,128)(2,1)S(1)}, f32[384,896]{1,0:T(8,128)}, f32[384,896]{1,0:T(8,128)}, f32[384,896]{1,0:T(8,128)}, /*index=5*/f32[384,896]{1,0:T(8,128)S(1)}) fusion(f32[384,896]{1,0:T(8,128)S(1)} %fusion.31, bf16[384,4096]{1,0:T(8,128)(2,1)S(1)} %constant_dynamic-update-slice_fusion, ...), kind=kOutput, calls=%fused_computation.20 | convolution fusion | flops 2822012928 | bytes 19431424 | tf_op jit(solution)/shard_map/dot_general | solution.py:492
  16.4 7.2 %convolution_convert_fusion.refs_0_ = bf16[384,4096]{1,0:T(8,128)(2,1)S(1)} fusion(bf16[384,896]{1,0:T(8,128)(2,1)S(1)} %get-tuple-element.27.refs_3_, bf16[896,4096]{1,0:T(8,128)(2,1)} %param.13), kind=kOutput, calls=%fused_computation | convolution fusion | flops 2820145152 | bytes 11173888 | tf_op jit(solution)/shard_map/dot_general | solution.py:492
  23.6 73.8 %shard_map.86 = (bf16[384,4096]{1,0:T(8,128)(2,1)S(1)}, bf16[384,512]{1,0:T(8,128)(2,1)S(1)}, bf16[1536,512]{1,0:T(8,128)(2,1)S(1)}, bf16[1536,896]{1,0:T(8,128)(2,1)S(1)}, bf16[1536,512]{1,0:T(8,128)(2,1)S(1)}) custom-call(bf16[384,4096]{1,0:T(8,128)(2,1)S(1)} %convolution_convert_fusion.refs_0_, bf16[384,512]{1,0:T(8,128)(2,1)S(1)} %get-tuple-element.38.refs_1_, ...), custom_call_target="tpu_custom_call" | custom-call | tf_op jit(solution)/shard_map/pallas_call | solution.py:305
  97.4 8.9 %multiply_convert_fusion.5 = (bf16[384,896]{1,0:T(8,128)(2,1)S(1)}, bf16[384,896]{1,0:T(8,128)(2,1)S(1)}, f32[384,896]{1,0:T(8,128)}) fusion(f32[384,896]{1,0:T(8,128)S(1)} %fusion.31, f32[384,896]{1,0:T(8,128)S(1)} %get-tuple-element.34, bf16[384,4096]{1,0:T(8,128)(2,1)S(1)} %get-tuple-element.16, bf16[896,4096]{1,0:T(8,128)(2,1)} %param.13), kind=kOutput, calls=%fused_computation.18 | convolution fusion | flops 2823045120 | bytes 15990784 | tf_op jit(solution)/shard_map/dot_general | solution.py:496
  106.3 0.1 pad_maximum_fusion.1.refs_1_
  106.4 0.8 convolution_convert_fusion.3
  107.2 0.8 fusion.32
  108.1 0.1 slice.182
  108.1 1.4 convolution_convert_fusion.2
  109.6 0.3 pad_maximum_fusion.refs_0_
  109.8 66.7 %shard_map.87 = (bf16[1024,1536]{1,0:T(8,128)(2,1)S(1)}, bf16[1536,1792]{1,0:T(8,128)(2,1)S(1)}) custom-call(bf16[1024,1536]{1,0:T(8,128)(2,1)S(1)} %pad_maximum_fusion.refs_0_, bf16[384,1792]{1,0:T(8,128)(2,1)S(1)} %pad_maximum_fusion.1.refs_1_), custom_call_target="tpu_custom_call" | custom-call | tf_op jit(solution)/shard_map/pallas_call | solution.py:305
  176.5 3.7 %select_reduce_fusion = (f32[384]{0:T(512)S(1)}, f32[384]{0:T(512)S(1)}, bf16[384,1536]{1,0:T(8,128)(2,1)}) fusion(pred[1536]{0:T(1024)(128)(4,1)S(1)} %fusion.22, f32[384,1536]{1,0:T(8,128)S(1)} %fusion.32, bf16[1024,1536]{1,0:T(8,128)(2,1)S(1)} %get-tuple-element.17, bf16[1536,1792]{1,0:T(8,128)(2,1)S(1)} %get-tuple-element.18, ...), kind=kOutput, calls=%fused_computation.7 | convolution fusion | flops 2122579200 | bytes 12784128 | tf_op jit(solution)/shard_map/dot_general | solution.py:496
  180.3 0.7 slice_reduce_fusion.2
  180.9 0.6 slice_reduce_fusion.1
  181.5 0.6 slice_reduce_fusion
  182.1 2.0 select_maximum_fusion
  184.1 0.1 broadcast_in_dim.41.refs_0_
  184.2 9.1 %shard_map.88 = f32[8,128]{1,0:T(8,128)S(1)} custom-call(f32[8,128]{1,0:T(8,128)S(1)} %broadcast_in_dim.41.refs_0_), custom_call_target="tpu_custom_call" | custom-call | tf_op jit(solution)/shard_map/pallas_call | solution.py:305
  193.3 0.6 fusion.30
  196.6 0.0 slice-start.4
  196.6 2.4 fusion.10.refs_1_
  199.0 0.2 copy-done.4
  199.2 4.4 %fusion.9 = f32[256,1792]{1,0:T(8,128)S(1)} fusion(bf16[1536,1792]{1,0:T(8,128)(2,1)} %copy-done.5, f32[1536]{0:T(1024)S(1)} %broadcast_select_fusion, bf16[1024,1536]{1,0:T(8,128)(2,1)S(1)} %copy-done.4), kind=kOutput, calls=%fused_computation.36 | convolution fusion | flops 1410465792 | bytes 8134656 | tf_op jit(solution)/shard_map/dot_general | solution.py:492
  203.7 0.7 slice-done.5
  204.4 2.5 convolution_convert_fusion.1.refs_0_
  206.9 0.1 slice.181.refs_2_
  206.9 66.5 %shard_map.89 = (bf16[256,4096]{1,0:T(8,128)(2,1)S(1)}, bf16[256,512]{1,0:T(8,128)(2,1)S(1)}, bf16[256,1536]{1,0:T(8,128)(2,1)S(1)}) custom-call(bf16[256,4096]{1,0:T(8,128)(2,1)S(1)} %convolution_convert_fusion.1.refs_0_, f32[256,512]{1,0:T(8,128)S(1)} %fusion.10.refs_1_, bf16[256,1536]{1,0:T(8,128)(2,1)S(1)} %slice.181.refs_2_), custom_call_target="tpu_custom_call" | custom-call | tf_op jit(solution)/shard_map/pallas_call | solution.py:305
  273.4 0.6 convolution_add_fusion.2.refs_1_
  274.0 0.0 slice-start.2
  274.0 5.6 %fusion.33 = f32[256,896]{1,0:T(8,128)S(1)} fusion(bf16[256,4096]{1,0:T(8,128)(2,1)S(1)} %get-tuple-element.19, bf16[896,4096]{1,0:T(8,128)(2,1)} %param.13), kind=kOutput, calls=%fused_computation.75 | convolution fusion | flops 1879048192 | bytes 10354688 | tf_op jit(solution)/shard_map/dot_general | solution.py:496
  279.6 1.0 convolution_add_fusion.1
  280.7 0.3 copy-done.10
  281.0 0.4 copy-done.14
  281.4 5.0 %fusion.18 = f32[256,4096]{1,0:T(8,128)S(1)} fusion(bf16[4096,896]{1,0:T(8,128)(2,1)S(1)} %bitcast.33, f32[384,896]{1,0:T(8,128)} %get-tuple-element.28, f32[384,896]{1,0:T(8,128)} %copy-done.16, f32[384,896]{1,0:T(8,128)} %get-tuple-element.30, f32[256,896]{1,0:T(8,128)S(1)} %convolution_add_fusion.1, f32[384,896]{1,0:T(8,128)S(1)} %copy-done.10, ...), kind=kOutput, calls=%fused_computation.46 | convolution fusion | flops 1882488832 | bytes 19791872 | tf_op jit(solution)/shard_map/dot_general | solution.py:496
  286.4 0.0 copy-start.1
  286.4 6.3 %fusion.refs_0_ = bf16[256,4096]{1,0:T(8,128)(2,1)S(1)} fusion(f32[256,4096]{1,0:T(8,128)S(1)} %fusion.18, bf16[4096,896]{1,0:T(8,128)(2,1)} %param.12, f32[256,896]{1,0:T(8,128)S(1)} %convolution_add_fusion.1, f32[384,896]{1,0:T(8,128)S(1)} %copy-done.10, f32[384,896]{1,0:T(8,128)} %get-tuple-element.29, f32[256,1792]{1,0:T(8,128)} %copy-done.11, ...), kind=kOutput, calls=%fused_computation.3 | convolution fusion | flops 1882292224 | bytes 18219008 | tf_op jit(solution)/shard_map/dot_general | solution.py:496
  292.7 34.2 %shard_map.90 = f32[256,512]{1,0:T(8,128)S(1)} custom-call(bf16[256,4096]{1,0:T(8,128)(2,1)S(1)} %fusion.refs_0_, f32[256,512]{1,0:T(8,128)S(1)} %convolution_add_fusion.2.refs_1_), custom_call_target="tpu_custom_call" | custom-call | tf_op jit(solution)/shard_map/pallas_call | solution.py:305
  326.9 0.8 copy.11
  (42 shorter events, 0.1 us)
Async XLA Ops:
  0.6 1.6 copy-start
  3.2 4.0 %copy-start.8 = (bf16[4096,896]{1,0:T(8,128)(2,1)S(1)}, bf16[4096,896]{1,0:T(8,128)(2,1)}, u32[]{:S(2)}) copy-start(bf16[4096,896]{1,0:T(8,128)(2,1)} %param.12) | copy-start | bytes 22020100
  6.7 3.9 %slice-start = ((s8[7340032]{0:T(1024)(128)(4,1)}), s8[4194304]{0:T(1024)(128)(4,1)S(1)}, s32[]{:S(2)}) async-start(s8[7340032]{0:T(1024)(128)(4,1)} %bitcast.30), calls=%async_computation | async-start | bytes 8388608
  7.2 3.4 %slice-start.1 = ((s8[7340032]{0:T(1024)(128)(4,1)}), s8[3145728]{0:T(1024)(128)(4,1)S(1)}, s32[]{:S(2)}) async-start(s8[7340032]{0:T(1024)(128)(4,1)} %bitcast.30), calls=%async_computation.1 | async-start | bytes 6291456
  10.6 86.7 %copy-start.12 = (f32[384,896]{1,0:T(8,128)}, f32[384,896]{1,0:T(8,128)S(1)}, u32[]{:S(2)}) copy-start(f32[384,896]{1,0:T(8,128)S(1)} %fusion.31) | copy-start | bytes 4128772
  16.4 81.0 %copy-start.16 = (f32[384,896]{1,0:T(8,128)}, f32[384,896]{1,0:T(8,128)S(1)}, u32[]{:S(2)}) copy-start(f32[384,896]{1,0:T(8,128)S(1)} %get-tuple-element.34) | copy-start | bytes 4128772
  97.3 9.1 %copy-start.6 = (bf16[1536,512]{1,0:T(8,128)(2,1)}, bf16[1536,512]{1,0:T(8,128)(2,1)S(1)}, u32[]{:S(2)}) copy-start(bf16[1536,512]{1,0:T(8,128)(2,1)S(1)} %get-tuple-element.12) | copy-start | bytes 4718596
  97.4 9.9 %copy-start.2 = (bf16[1536,512]{1,0:T(8,128)(2,1)}, bf16[1536,512]{1,0:T(8,128)(2,1)S(1)}, u32[]{:S(2)}) copy-start(bf16[1536,512]{1,0:T(8,128)(2,1)S(1)} %get-tuple-element.15) | copy-start | bytes 4718596
  176.5 3.8 %copy-start.3 = (bf16[1024,1536]{1,0:T(8,128)(2,1)}, bf16[1024,1536]{1,0:T(8,128)(2,1)S(1)}, u32[]{:S(2)}) copy-start(bf16[1024,1536]{1,0:T(8,128)(2,1)S(1)} %get-tuple-element.17) | copy-start | bytes 9437188
  176.5 3.8 %copy-start.5 = (bf16[1536,1792]{1,0:T(8,128)(2,1)}, bf16[1536,1792]{1,0:T(8,128)(2,1)S(1)}, u32[]{:S(2)}) copy-start(bf16[1536,1792]{1,0:T(8,128)(2,1)S(1)} %get-tuple-element.18) | copy-start | bytes 16515076
  196.6 2.6 copy-start.4
  196.6 7.0 %slice-start.4 = ((s8[7340032]{0:T(1024)(128)(4,1)}), s8[4194304]{0:T(1024)(128)(4,1)S(1)}, s32[]{:S(2)}) async-start(s8[7340032]{0:T(1024)(128)(4,1)} %bitcast.34), calls=%async_computation.4 | async-start | bytes 8388608
  199.2 4.4 %copy-start.9 = (f32[384,896]{1,0:T(8,128)S(1)}, f32[384,896]{1,0:T(8,128)}, u32[]{:S(2)}) copy-start(f32[384,896]{1,0:T(8,128)} %get-tuple-element.26) | copy-start | bytes 4128772
  199.2 4.5 %copy-start.13 = (f32[384,896]{1,0:T(8,128)S(1)}, f32[384,896]{1,0:T(8,128)}, u32[]{:S(2)}) copy-start(f32[384,896]{1,0:T(8,128)} %copy-done.12) | copy-start | bytes 4128772
  199.2 4.5 %copy-start.15 = (f32[384,896]{1,0:T(8,128)S(1)}, f32[384,896]{1,0:T(8,128)}, u32[]{:S(2)}) copy-start(f32[384,896]{1,0:T(8,128)} %get-tuple-element.29) | copy-start | bytes 4128772
  199.2 5.2 %slice-start.5 = ((s8[7340032]{0:T(1024)(128)(4,1)}), s8[3145728]{0:T(1024)(128)(4,1)S(1)}, s32[]{:S(2)}) async-start(s8[7340032]{0:T(1024)(128)(4,1)} %bitcast.34), calls=%async_computation.5 | async-start | bytes 6291456
  203.6 3.2 copy-start.11
  204.4 2.5 copy-start.17
  206.9 66.5 %copy-start.7 = (bf16[1536,512]{1,0:T(8,128)(2,1)S(1)}, bf16[1536,512]{1,0:T(8,128)(2,1)}, u32[]{:S(2)}) copy-start(bf16[1536,512]{1,0:T(8,128)(2,1)} %copy-done.6) | copy-start | bytes 4718596
  274.0 6.6 %slice-start.2 = ((s8[7340032]{0:T(1024)(128)(4,1)}), s8[4194304]{0:T(1024)(128)(4,1)S(1)}, s32[]{:S(2)}) async-start(s8[7340032]{0:T(1024)(128)(4,1)} %bitcast.32), calls=%async_computation.2 | async-start | bytes 8388608
  274.0 6.6 %slice-start.3 = ((s8[7340032]{0:T(1024)(128)(4,1)}), s8[3145728]{0:T(1024)(128)(4,1)S(1)}, s32[]{:S(2)}) async-start(s8[7340032]{0:T(1024)(128)(4,1)} %bitcast.32), calls=%async_computation.3 | async-start | bytes 6291456
  279.6 1.3 copy-start.10
  279.6 1.7 copy-start.14
  286.4 41.3 %copy-start.1 = (bf16[256,4096]{1,0:T(8,128)(2,1)S(1)}, bf16[256,4096]{1,0:T(8,128)(2,1)}, u32[]{:S(2)}) copy-start(bf16[256,4096]{1,0:T(8,128)(2,1)} %param.10) | copy-start | bytes 6291460

commit v4 on v3

--- a/solution.py
+++ b/solution.py
@@ -23,8 +23,12 @@
 
 
 def over_rows(count, body, init=0):
+    size = next(size for size in (64, 32, STEP) if count % size == 0)
     return lax.fori_loop(
-        0, count // STEP, lambda i, c: body(pl.ds(pl.multiple_of(i * STEP, STEP), STEP), i, c), init
+        0,
+        count // size,
+        lambda i, c: body(pl.ds(pl.multiple_of(i * size, size), size), i * size, c),
+        init,
     )
 
 
@@ -218,7 +222,7 @@
         g, last = self.group, self.groups - 1
         target = piece(full, self.me)
         self.keep(own, target)
-        near = [(self.start(own, target, self.twin), None)]
+        near = []
         hops = []
         for t in range(last):
             for way, device in ((1, self.above), (-1, self.below)):
@@ -233,6 +237,8 @@
             mine = [hop for hop in hops if hop[0] == t]
             for _, copy, sends, _, _ in mine:
                 pl.when(sends)(copy.start)
+            if t == 0:
+                near.append((self.start(own, target, self.twin), None))
             if t == 0 and between is not None:
                 between()
             for _, copy, _, gets, onward in mine:
@@ -327,7 +333,7 @@
         apply = ex.reduce_close(part, piece, twin, half, far, opened, sent)
 
         def loss(total, rows, i, c):
-            share = jnp.where(i * STEP < n_tgt, tgt_share, poi_share)
+            share = jnp.where(i < n_tgt, tgt_share, poi_share)
             value = x[rows, :].astype(F32) + total - goal[rows, :].astype(F32)
             own[rows, :] = (value * share).astype(BF)
             return c
@@ -390,17 +396,36 @@
     )
 
 
-def sum_exchange(n, n_dp, tile):
-    def body(ex, tile, out, tiles, row_tiles):
+def coef_exchange(n, n_dp, n_tgt, with_tgt, with_poi):
+    split = n_tgt // 128
+
+    def body(ex, with_tgt, with_poi, out, tiles, row_tiles):
         ex.greet(True, True, every=True)
-        tiles[ex.me] = tile[...]
-        out[...] = ex.sum_tiles(tiles, row_tiles)
+        tiles[ex.me] = jnp.concatenate(
+            [
+                jnp.sum(with_tgt[:split], axis=0, keepdims=True),
+                jnp.sum(with_poi[split:], axis=0, keepdims=True),
+                jnp.sum(with_tgt[split:], axis=0, keepdims=True),
+                jnp.zeros((5, 128), F32),
+            ],
+            axis=0,
+        )
+        sums = jnp.sum(ex.sum_tiles(tiles, row_tiles), axis=1, keepdims=True)
+        sums = jnp.broadcast_to(sums, (8, 128))
+        length_tgt = jnp.sqrt(sums[0:1] + EPSILON)
+        length_poi = jnp.sqrt(sums[1:2] + EPSILON)
+        denom = length_tgt * length_poi
+        cross = sums[2:3]
+        out[0:1] = -1.0 / denom
+        out[1:2] = cross / (denom * length_poi * length_poi)
+        out[2:3] = 1.0 - cross / denom
+        out[3:8] = jnp.zeros((5, 128), F32)
 
     return communicate(
         body, n, n_dp, (n - 1) + (n_dp - 1), 0,
-        [(tile.shape, F32, True)],
-        [(tile, True)],
-        [pltpu.VMEM((n,) + tile.shape, F32), pltpu.VMEM((n_dp,) + tile.shape, F32)], 3,
+        [((8, 128), F32, True)],
+        [(with_tgt, True), (with_poi, True)],
+        [pltpu.VMEM((n, 8, 128), F32), pltpu.VMEM((n_dp, 8, 128), F32)], 3,
     )[0]
 
 
@@ -458,9 +483,9 @@
         def store(total, rows, i, c):
             value = (total + extra[rows, :]) * scale
             out[rows, :] = value
-            return c + value * value
-
-        squares = apply(store, height, jnp.zeros((STEP, width), F32))
+            return c + jnp.sum((value * value).reshape(-1, 8, width), axis=0)
+
+        squares = apply(store, height, jnp.zeros((8, width), F32))
         tiles[ex.me] = jnp.broadcast_to(jnp.sum(squares), (8, 128))
         summed = ex.sum_tiles(tiles, row_tiles)
         factor = lax.rsqrt(jnp.max(summed) / entries + EPSILON)
@@ -551,19 +576,11 @@
     both = gram_x.astype(F32) * gram_b_part + gram_h.astype(F32) * gram_e_part
     sum_tgt = jnp.sum(jnp.where(is_tgt_all[None, :], both, 0.0), axis=1)
     sum_poi = jnp.sum(jnp.where(is_tgt_all[None, :], 0.0, both), axis=1)
-    sums = jnp.stack(
-        [jnp.sum(sum_tgt[:n_tgt]), jnp.sum(sum_poi[n_tgt:]), jnp.sum(sum_tgt[n_tgt:])]
-    )
-    tile = jnp.broadcast_to(jnp.pad(sums, (0, 5))[:, None], (8, 128))
-    sums = sum_exchange(n_fsdp, n_dp, tile)[:, 0]
-    norm_tt, norm_pp, cross_tp = sums[0], sums[1], sums[2]
-    length_tgt = jnp.sqrt(norm_tt + EPSILON)
-    length_poi = jnp.sqrt(norm_pp + EPSILON)
-    denom = length_tgt * length_poi
-    alignment = 1.0 - cross_tp / denom
-    coef_tgt = -1.0 / denom
-    coef_poi = cross_tp / (denom * length_poi * length_poi)
-    coef = jnp.where(is_tgt_all, coef_tgt, coef_poi)[None, :]
+    coefs = coef_exchange(
+        n_fsdp, n_dp, n_tgt, sum_tgt.reshape(-1, 128), sum_poi.reshape(-1, 128)
+    )
+    alignment = coefs[2, 0]
+    coef = jnp.where(is_tgt_all, coefs[0, 0], coefs[1, 0])[None, :]
 
     def weigh(gram):
         return (gram.astype(F32) * coef).astype(BF)

time: 329 us -> 316 us (0.960)
  matrix products: 59.7 us -> 53.9 us
  between operations: 4.97 us -> 1.04 us
    dot_general x8, matrix products: 27.1 us -> 22.3 us  [matmul(): return jnp.dot(left, right, preferred_element_type=F32)]
    unnamed x50 -> x36, local copies, waits for them, and re-layouts: 5.94 us -> 7.15 us
where the time goes in v4:
time: 316 us
  Pallas kernels  248 us (78%)
  matrix products  53.9 us (17%)
  local copies, waits for them, and re-layouts  10.9 us (3%)
    pallas_call x5, Pallas kernels, communicate(): pl.pallas_call(kernel, out_shape=[jax.ShapeDtypeStruct(shape, kind) for s...  248 us
    dot_general x8, matrix products, inner_cols(): lax.dot_general(left, right, (((1,), (1,)), ((), ())), preferred_element_...  31.6 us
    dot_general x8, matrix products, matmul(): return jnp.dot(left, right, preferred_element_type=F32)  22.3 us
    unnamed x36, local copies, waits for them, and re-layouts  7.15 us

profile of v4, /device:TPU:0, one launch (start us, length us, event | category | flops | bytes accessed | tf_op | source)
XLA Modules:
  0.0 316.0 jit_solution(11508244477967376382)
XLA Ops:
  0.6 0.0 copy-start
  0.7 1.6 copy-done
  2.2 0.9 constant_dynamic-slice_fusion.1
  3.2 0.0 copy-start.2
  3.2 1.5 constant_dynamic-update-slice_fusion.1
  4.7 2.1 constant_dynamic-update-slice_fusion
  6.7 0.0 slice-start
  6.7 0.1 pad_maximum_fusion.2
  6.8 0.4 copy-done.2
  7.2 3.4 %fusion.31 = f32[384,896]{1,0:T(8,128)S(1)} fusion(bf16[384,4096]{1,0:T(8,128)(2,1)S(1)} %constant_dynamic-update-slice_fusion, bf16[4096,896]{1,0:T(8,128)(2,1)S(1)} %copy-done.2), kind=kOutput, calls=%fused_computation.67 | convolution fusion | flops 2818572288 | bytes 11862016 | tf_op jit(solution)/shard_map/dot_general | solution.py:517
  10.7 0.0 slice-done
  10.7 0.0 slice-done.1
  10.7 5.5 %add_multiply_fusion = (f32[384,896]{1,0:T(8,128)S(1)}, bf16[384,896]{1,0:T(8,128)(2,1)S(1)}, f32[384,896]{1,0:T(8,128)}, f32[384,896]{1,0:T(8,128)}, f32[384,896]{1,0:T(8,128)}, /*index=5*/f32[384,896]{1,0:T(8,128)S(1)}) fusion(f32[384,896]{1,0:T(8,128)S(1)} %fusion.31, bf16[384,4096]{1,0:T(8,128)(2,1)S(1)} %constant_dynamic-update-slice_fusion, ...), kind=kOutput, calls=%fused_computation.20 | convolution fusion | flops 2822012928 | bytes 19431424 | tf_op jit(solution)/shard_map/dot_general | solution.py:517
  16.2 7.2 %convolution_convert_fusion.refs_0_ = bf16[384,4096]{1,0:T(8,128)(2,1)S(1)} fusion(bf16[384,896]{1,0:T(8,128)(2,1)S(1)} %get-tuple-element.27.refs_3_, bf16[896,4096]{1,0:T(8,128)(2,1)} %param.13), kind=kOutput, calls=%fused_computation | convolution fusion | flops 2820145152 | bytes 11173888 | tf_op jit(solution)/shard_map/dot_general | solution.py:517
  23.4 73.2 %shard_map.86 = (bf16[384,4096]{1,0:T(8,128)(2,1)S(1)}, bf16[384,512]{1,0:T(8,128)(2,1)S(1)}, bf16[1536,512]{1,0:T(8,128)(2,1)S(1)}, bf16[1536,896]{1,0:T(8,128)(2,1)S(1)}, bf16[1536,512]{1,0:T(8,128)(2,1)S(1)}) custom-call(bf16[384,4096]{1,0:T(8,128)(2,1)S(1)} %convolution_convert_fusion.refs_0_, bf16[384,512]{1,0:T(8,128)(2,1)S(1)} %get-tuple-element.38.refs_1_, ...), custom_call_target="tpu_custom_call" | custom-call | tf_op jit(solution)/shard_map/pallas_call | solution.py:311
  96.6 7.8 %multiply_convert_fusion.5 = (bf16[384,896]{1,0:T(8,128)(2,1)S(1)}, bf16[384,896]{1,0:T(8,128)(2,1)S(1)}, f32[384,896]{1,0:T(8,128)}) fusion(f32[384,896]{1,0:T(8,128)S(1)} %fusion.31, f32[384,896]{1,0:T(8,128)S(1)} %get-tuple-element.34, bf16[384,4096]{1,0:T(8,128)(2,1)S(1)} %get-tuple-element.16, bf16[896,4096]{1,0:T(8,128)(2,1)} %param.13), kind=kOutput, calls=%fused_computation.18 | convolution fusion | flops 2823045120 | bytes 15990784 | tf_op jit(solution)/shard_map/dot_general | solution.py:521
  104.4 0.1 pad_maximum_fusion.1.refs_1_
  104.5 0.8 convolution_convert_fusion.3
  105.3 1.4 convolution_convert_fusion.2
  106.8 0.8 fusion.32
  107.6 0.1 slice.160
  107.7 0.3 pad_maximum_fusion.refs_0_
  107.9 66.5 %shard_map.87 = (bf16[1024,1536]{1,0:T(8,128)(2,1)S(1)}, bf16[1536,1792]{1,0:T(8,128)(2,1)S(1)}) custom-call(bf16[1024,1536]{1,0:T(8,128)(2,1)S(1)} %pad_maximum_fusion.refs_0_, bf16[384,1792]{1,0:T(8,128)(2,1)S(1)} %pad_maximum_fusion.1.refs_1_), custom_call_target="tpu_custom_call" | custom-call | tf_op jit(solution)/shard_map/pallas_call | solution.py:311
  174.4 3.8 %select_reduce_fusion = (f32[384]{0:T(512)S(1)}, f32[384]{0:T(512)S(1)}, bf16[384,1536]{1,0:T(8,128)(2,1)S(1)}) fusion(pred[1536]{0:T(1024)(128)(4,1)S(1)} %fusion.22, f32[384,1536]{1,0:T(8,128)S(1)} %fusion.32, bf16[1024,1536]{1,0:T(8,128)(2,1)S(1)} %get-tuple-element.17, bf16[1536,1792]{1,0:T(8,128)(2,1)S(1)} %get-tuple-element.18, ...), kind=kOutput, calls=%fused_computation.7 | convolution fusion | flops 2122579200 | bytes 12784128 | tf_op jit(solution)/shard_map/dot_general | solution.py:521
  178.2 9.3 %shard_map.88 = f32[8,128]{1,0:T(8,128)S(1)} custom-call(f32[3,128]{1,0:T(4,128)S(1)} %bitcast.30, f32[3,128]{1,0:T(4,128)S(1)} %bitcast.29), custom_call_target="tpu_custom_call" | custom-call | tf_op jit(solution)/shard_map/pallas_call | solution.py:311
  187.5 0.6 fusion.30
  188.1 1.3 broadcast_select_fusion
  189.4 0.0 slice-start.4
  189.4 0.6 fusion.10.refs_1_
  190.0 0.0 slice-start.5
  190.0 1.6 fusion.9
  191.7 0.5 copy-done.8
  192.2 0.4 copy-done.9
  192.6 1.6 slice-done.5
  194.2 2.5 convolution_convert_fusion.1.refs_0_
  196.7 0.1 slice.159.refs_2_
  196.7 66.8 %shard_map.89 = (bf16[256,4096]{1,0:T(8,128)(2,1)S(1)}, bf16[256,512]{1,0:T(8,128)(2,1)S(1)}, bf16[256,1536]{1,0:T(8,128)(2,1)S(1)}) custom-call(bf16[256,4096]{1,0:T(8,128)(2,1)S(1)} %convolution_convert_fusion.1.refs_0_, f32[256,512]{1,0:T(8,128)S(1)} %fusion.10.refs_1_, bf16[256,1536]{1,0:T(8,128)(2,1)S(1)} %slice.159.refs_2_), custom_call_target="tpu_custom_call" | custom-call | tf_op jit(solution)/shard_map/pallas_call | solution.py:311
  263.5 0.6 convolution_add_fusion.2.refs_1_
  264.1 0.0 slice-start.2
  264.1 0.0 slice-start.3
  264.1 5.6 %fusion.33 = f32[256,896]{1,0:T(8,128)S(1)} fusion(bf16[256,4096]{1,0:T(8,128)(2,1)S(1)} %get-tuple-element.19, bf16[896,4096]{1,0:T(8,128)(2,1)} %param.13), kind=kOutput, calls=%fused_computation.69 | convolution fusion | flops 1879048192 | bytes 10354688 | tf_op jit(solution)/shard_map/dot_general | solution.py:521
  269.8 1.0 convolution_add_fusion.1
  270.8 0.3 copy-done.3
  271.1 5.2 %fusion.18 = f32[256,4096]{1,0:T(8,128)S(1)} fusion(bf16[4096,896]{1,0:T(8,128)(2,1)S(1)} %bitcast.34, f32[384,896]{1,0:T(8,128)} %get-tuple-element.28, f32[384,896]{1,0:T(8,128)} %copy-done.10, f32[384,896]{1,0:T(8,128)} %get-tuple-element.30, f32[256,896]{1,0:T(8,128)S(1)} %convolution_add_fusion.1, f32[384,896]{1,0:T(8,128)S(1)} %copy-done.3, ...), kind=kOutput, calls=%fused_computation.46 | convolution fusion | flops 1882488832 | bytes 19791872 | tf_op jit(solution)/shard_map/dot_general | solution.py:521
  276.3 0.0 copy-start.1
  276.3 6.2 %fusion.refs_0_ = bf16[256,4096]{1,0:T(8,128)(2,1)S(1)} fusion(f32[256,4096]{1,0:T(8,128)S(1)} %fusion.18, bf16[4096,896]{1,0:T(8,128)(2,1)} %param.12, f32[256,896]{1,0:T(8,128)S(1)} %convolution_add_fusion.1, f32[384,896]{1,0:T(8,128)S(1)} %copy-done.4, f32[384,896]{1,0:T(8,128)} %get-tuple-element.29, f32[256,1792]{1,0:T(8,128)} %copy-done.5, ...), kind=kOutput, calls=%fused_computation.3 | convolution fusion | flops 1882292224 | bytes 18219008 | tf_op jit(solution)/shard_map/dot_general | solution.py:521
  282.6 32.7 %shard_map.90 = f32[256,512]{1,0:T(8,128)S(1)} custom-call(bf16[256,4096]{1,0:T(8,128)(2,1)S(1)} %fusion.refs_0_, f32[256,512]{1,0:T(8,128)S(1)} %convolution_add_fusion.2.refs_1_), custom_call_target="tpu_custom_call" | custom-call | tf_op jit(solution)/shard_map/pallas_call | solution.py:311
  315.2 0.8 copy.11
  (23 shorter events, 0.1 us)
Async XLA Ops:
  0.6 1.6 copy-start
  3.2 4.0 %copy-start.2 = (bf16[4096,896]{1,0:T(8,128)(2,1)S(1)}, bf16[4096,896]{1,0:T(8,128)(2,1)}, u32[]{:S(2)}) copy-start(bf16[4096,896]{1,0:T(8,128)(2,1)} %param.12) | copy-start | bytes 22020100
  6.7 3.9 %slice-start = ((s8[7340032]{0:T(1024)(128)(4,1)}), s8[4194304]{0:T(1024)(128)(4,1)S(1)}, s32[]{:S(2)}) async-start(s8[7340032]{0:T(1024)(128)(4,1)} %bitcast.31), calls=%async_computation | async-start | bytes 8388608
  7.2 3.5 %slice-start.1 = ((s8[7340032]{0:T(1024)(128)(4,1)}), s8[3145728]{0:T(1024)(128)(4,1)S(1)}, s32[]{:S(2)}) async-start(s8[7340032]{0:T(1024)(128)(4,1)} %bitcast.31), calls=%async_computation.1 | async-start | bytes 6291456
  10.7 85.9 %copy-start.7 = (f32[384,896]{1,0:T(8,128)}, f32[384,896]{1,0:T(8,128)S(1)}, u32[]{:S(2)}) copy-start(f32[384,896]{1,0:T(8,128)S(1)} %fusion.31) | copy-start | bytes 4128772
  16.2 80.4 %copy-start.10 = (f32[384,896]{1,0:T(8,128)}, f32[384,896]{1,0:T(8,128)S(1)}, u32[]{:S(2)}) copy-start(f32[384,896]{1,0:T(8,128)S(1)} %get-tuple-element.34) | copy-start | bytes 4128772
  104.4 2.3 copy-start.6
  189.4 2.2 slice-start.4
  190.0 2.2 copy-start.8
  190.0 2.6 copy-start.9
  190.0 4.2 %slice-start.5 = ((s8[7340032]{0:T(1024)(128)(4,1)}), s8[3145728]{0:T(1024)(128)(4,1)S(1)}, s32[]{:S(2)}) async-start(s8[7340032]{0:T(1024)(128)(4,1)} %bitcast.35), calls=%async_computation.5 | async-start | bytes 6291456
  191.6 5.0 %copy-start.5 = (f32[256,1792]{1,0:T(8,128)}, f32[256,1792]{1,0:T(8,128)S(1)}, u32[]{:S(2)}) copy-start(f32[256,1792]{1,0:T(8,128)S(1)} %fusion.9) | copy-start | bytes 5505028
  264.1 6.6 %slice-start.2 = ((s8[7340032]{0:T(1024)(128)(4,1)}), s8[4194304]{0:T(1024)(128)(4,1)S(1)}, s32[]{:S(2)}) async-start(s8[7340032]{0:T(1024)(128)(4,1)} %bitcast.33), calls=%async_computation.2 | async-start | bytes 8388608
  264.1 6.6 %slice-start.3 = ((s8[7340032]{0:T(1024)(128)(4,1)}), s8[3145728]{0:T(1024)(128)(4,1)S(1)}, s32[]{:S(2)}) async-start(s8[7340032]{0:T(1024)(128)(4,1)} %bitcast.33), calls=%async_computation.3 | async-start | bytes 6291456
  269.7 1.3 copy-start.3
  271.1 5.2 %copy-start.4 = (f32[384,896]{1,0:T(8,128)S(1)}, f32[384,896]{1,0:T(8,128)}, u32[]{:S(2)}) copy-start(f32[384,896]{1,0:T(8,128)} %get-tuple-element.35) | copy-start | bytes 4128772
  276.3 39.7 %copy-start.1 = (bf16[256,4096]{1,0:T(8,128)(2,1)S(1)}, bf16[256,4096]{1,0:T(8,128)(2,1)}, u32[]{:S(2)}) copy-start(bf16[256,4096]{1,0:T(8,128)(2,1)} %param.10) | copy-start | bytes 6291460
